TPU v7x, 256 devices: a whole 4x4x8 slice. The times are simulated.
256 devices in a mesh: expert: 8 (over z_hi, x), row: 32 (over y, z_lo, core).
Axes of the slice: x: 4, y: 4, z: 8 (z_hi: 2, z_lo: 4; z = z_hi * 4 + z_lo), core: 2. Of those that a mesh axis runs over, the one named last changes fastest.
Arguments:
- momentum: bfloat16 [256, 2048, 768], P('expert', 'row'), may hold values from -6 to 6
- gradient: bfloat16 [256, 2048, 768], P('expert', 'row'), may hold values from -6 to 6
- owners: int32 [8, 32], P('expert'), may hold values from 0 to 31, as said below
Outputs:
- new_momentum: bfloat16 [256, 2048, 768], P('expert', 'row')
- update: bfloat16 [256, 2048, 768], P('expert', 'row')
- owner_scale: float32 [8, 32], P('expert', 'row')
Inputs may be any that keep to these rules, and one draw needn't show every extreme that they name: `owners`: in each row of the table every index appears exactly 1 times.
All inputs are finite; a program needn't handle non-finite values.
Results may differ from a plain program's by a relative error of at most 0.0085.
Values may be sent and summed in bfloat16 or wider, within the bound.
No kernel may reach another device: no remote copies, remote signals or barrier semaphores. Data moves between devices by JAX's collectives and lax.ppermute only.
A program may use at most 64 MiB of HBM per device.

v0:
```python
import functools
import math

import jax
import jax.numpy as jnp
from jax import lax
from jax.sharding import Mesh
from jax.sharding import PartitionSpec as P

D = 2048
FF = 768
ITERS = 2
ROW = ("row_0", "row_1", "row_2")
EXPERT_ROW = ("expert_0", "expert_1", "row_0", "row_1", "row_2")
EXPERT = ("expert_0", "expert_1")


quintic_one = 3.4445
quintic_two = -4.775
quintic_three = 2.0315
momentum_beta = 0.95
clip_rms = 0.25


def by_axis(x, axes):
    return functools.reduce(lax.psum, axes, x)


def newton_schulz(full_matrix):
    values = full_matrix.astype(jnp.float32)
    frobenius = jnp.sqrt(jnp.sum(values * values))
    iterate = (values / (frobenius + 1e-07)).astype(jnp.bfloat16)
    for step in range(ITERS):
        gram = lax.dot_general(
            iterate, iterate, (((0,), (0,)), ((), ())), preferred_element_type=jnp.float32
        ).astype(jnp.bfloat16)
        square = jnp.dot(gram, gram, preferred_element_type=jnp.float32)
        poly = (quintic_two * gram.astype(jnp.float32) + quintic_three * square).astype(
            jnp.bfloat16
        )
        product = jnp.dot(iterate, poly, preferred_element_type=jnp.float32)
        iterate = (quintic_one * iterate.astype(jnp.float32) + product).astype(jnp.bfloat16)
    update = (math.sqrt(D) * iterate.astype(jnp.float32)).astype(jnp.bfloat16)
    return (update, frobenius / math.sqrt(D * FF))


def orthogonalize_items(received):
    row_devices = received.shape[0]
    items = received.shape[1]
    row_count = received.shape[2]
    matrices = jnp.transpose(received, (1, 0, 2, 3)).reshape(items, row_devices * row_count, FF)
    updates, scales = lax.map(newton_schulz, matrices)
    updates = jnp.transpose(updates.reshape(items, row_devices, row_count, FF), (1, 0, 2, 3))
    return (updates, scales.reshape(1, items))


def local(momentum, gradient, owners):
    matrix_count = momentum.shape[0]
    row_count = momentum.shape[1]
    row_devices = lax.axis_size(ROW)
    per_owner = matrix_count // row_devices
    grad_f32 = gradient.astype(jnp.float32)
    local_sum = jnp.sum(grad_f32 * grad_f32)
    global_sum = by_axis(local_sum, EXPERT_ROW)
    entry_count = float(lax.axis_size(EXPERT) * matrix_count * row_devices * row_count * FF)
    factor = jnp.minimum(jnp.float32(1.0), clip_rms / jnp.sqrt(global_sum / entry_count + 1e-06))
    new_momentum = (momentum_beta * momentum.astype(jnp.float32) + factor * grad_f32).astype(
        jnp.bfloat16
    )
    owner_row = owners[0]
    positions = jnp.arange(matrix_count, dtype=jnp.int32)
    same = (owner_row[:, None] == owner_row[None, :]).astype(jnp.int32)
    earlier = (positions[None, :] < positions[:, None]).astype(jnp.int32)
    slot = jnp.sum(same * earlier, axis=1)
    code = owner_row * per_owner + slot
    placing = (code[None, :] == positions[:, None]).astype(jnp.bfloat16)
    flat_rows = new_momentum.reshape(matrix_count, row_count * FF)
    outgoing = jnp.dot(placing, flat_rows, preferred_element_type=jnp.float32).astype(jnp.bfloat16)
    outgoing = outgoing.reshape(row_devices, per_owner, row_count, FF)
    received = lax.all_to_all(outgoing, ROW, split_axis=0, concat_axis=0, tiled=True)
    owned, scales = orthogonalize_items(received)
    returned = lax.all_to_all(owned, ROW, split_axis=0, concat_axis=0, tiled=True)
    returned_flat = returned.reshape(matrix_count, row_count * FF)
    picked = lax.dot_general(
        placing, returned_flat, (((0,), (0,)), ((), ())), preferred_element_type=jnp.float32
    )
    updates = picked.astype(jnp.bfloat16).reshape(matrix_count, row_count, FF)
    return (new_momentum, updates, scales)


def solution(mesh):
    torus = Mesh(
        mesh.devices.reshape(2, 4, 4, 4, 2), ("expert_0", "expert_1", "row_0", "row_1", "row_2")
    )
    in_specs = (P(EXPERT, ROW, None), P(EXPERT, ROW, None), P(EXPERT, None))
    out_specs = (P(EXPERT, ROW, None), P(EXPERT, ROW, None), P(EXPERT, ROW))
    return jax.shard_map(local, mesh=torus, in_specs=in_specs, out_specs=out_specs, check_vma=False)
```

profile of v0, /device:TPU:1, one launch (start us, length us, event | category | flops | bytes accessed | tf_op | source)
XLA Modules:
  0.0 247.1 jit_solution(10202200447241300755)
XLA Ops:
  0.6 0.0 copy-start.1
  0.6 0.0 copy-start.3
  0.7 4.3 %fusion = f32[]{:T(128)} fusion(bf16[32,64,768]{2,1,0:T(8,128)(2,1)} %param.4), kind=kLoop, calls=%fused_computation.6 | loop fusion | flops 4718591 | bytes 3145732 | tf_op jit(solution)/shard_map/reduce_sum | solution.py:63
  4.9 10.7 %psum.35 = f32[]{:T(128)} all-reduce(f32[]{:T(128)} %fusion), channel_id=1, replica_groups=mesh['expert_0'=2,'expert_1'=4,'row_0'=4,'row_1'=4,'row_2'=2] {'expert_0'}, use_global_device_ids=true, to_apply=%region_1.0 | all-reduce | flops 1 | bytes 8 | tf_op jit(solution)/shard_map/psum | solution.py:26
  15.6 9.1 %psum.36 = f32[]{:T(128)} all-reduce(f32[]{:T(128)} %psum.35), channel_id=1, replica_groups=mesh['expert_0'=2,'expert_1'=4,'row_0'=4,'row_1'=4,'row_2'=2] {'expert_1'}, use_global_device_ids=true, to_apply=%region_2.0 | all-reduce | flops 1 | bytes 8 | tf_op jit(solution)/shard_map/psum | solution.py:26
  24.7 9.3 %psum.37 = f32[]{:T(128)} all-reduce(f32[]{:T(128)} %psum.36), channel_id=1, replica_groups=mesh['expert_0'=2,'expert_1'=4,'row_0'=4,'row_1'=4,'row_2'=2] {'row_0'}, use_global_device_ids=true, to_apply=%region_3.0 | all-reduce | flops 1 | bytes 8 | tf_op jit(solution)/shard_map/psum | solution.py:26
  34.0 10.0 %psum.38 = f32[]{:T(128)} all-reduce(f32[]{:T(128)} %psum.37), channel_id=1, replica_groups=mesh['expert_0'=2,'expert_1'=4,'row_0'=4,'row_1'=4,'row_2'=2] {'row_1'}, use_global_device_ids=true, to_apply=%region_4.0 | all-reduce | flops 1 | bytes 8 | tf_op jit(solution)/shard_map/psum | solution.py:26
  44.0 10.6 %psum.39 = f32[]{:T(128)} all-reduce(f32[]{:T(128)} %psum.38), channel_id=1, replica_groups=mesh['expert_0'=2,'expert_1'=4,'row_0'=4,'row_1'=4,'row_2'=2] {'row_2'}, use_global_device_ids=true, to_apply=%region_5.0 | all-reduce | flops 1 | bytes 8 | tf_op jit(solution)/shard_map/psum | solution.py:26
  55.3 0.0 copy-done.3
  55.4 0.2 select_reduce_fusion
  55.5 0.0 copy-done.1
  55.6 3.1 %fusion.2 = bf16[32,64,768]{2,1,0:T(8,128)(2,1)S(1)} fusion(bf16[32,64,768]{2,1,0:T(8,128)(2,1)S(1)} %copy-done.1, bf16[32,64,768]{2,1,0:T(8,128)(2,1)} %param.3, f32[]{:T(128)S(6)} %min_shard_map.3), kind=kLoop, calls=%fused_computation.8 | loop fusion | flops 9437184 | bytes 9437188 | tf_op jit(solution)/shard_map/convert_element_type | solution.py:67
  58.6 0.0 copy-start
  58.6 1.8 copy.12
  60.4 0.0 copy-done
  60.4 1.0 convolution_convert_fusion.1
  61.4 0.7 copy.13
  62.1 75.9 %all_to_all.10 = bf16[32,1,64,768]{3,2,1,0:T(8,128)(2,1)S(1)} all-to-all(bf16[32,1,64,768]{3,2,1,0:T(8,128)(2,1)S(1)} %bitcast.49), channel_id=1, replica_groups=mesh['expert_0'=2,'expert_1'=4,'row_0'=4,'row_1'=4,'row_2'=2] {'row_0','..., dimensions={0} | all-to-all | bytes 6291456 | tf_op jit(solution)/shard_map/all_to_all | solution.py:80
  138.0 2.2 fusion.3
  140.9 0.8 fusion.4
  141.7 0.0 copy-start.2
  141.8 3.7 %bitcast_convert_fusion = bf16[768,768]{1,0:T(8,128)(2,1)} fusion(bf16[32,1,64,768]{3,2,0,1:T(8,128)(2,1)S(1)} %fusion.4), kind=kOutput, calls=%fused_computation.16 | convolution fusion | flops 2416508928 | bytes 4325376 | tf_op jit(solution)/shard_map/while/body/eval_jaxpr/dot_general | solution.py:34
  145.4 0.0 copy-done.2
  145.4 7.6 %add_convert_fusion.1 = bf16[2048,768]{1,0:T(8,128)(2,1)S(1)} fusion(bf16[2048,768]{1,0:T(8,128)(2,1)} %bitcast.54, bf16[768,768]{1,0:T(8,128)(2,1)} %bitcast_convert_fusion), kind=kOutput, calls=%fused_computation.13 | convolution fusion | flops 3331129344 | bytes 7471104 | tf_op jit(solution)/shard_map/while/body/eval_jaxpr/dot_general | solution.py:41
  153.1 3.7 %convolution_convert_fusion.2 = bf16[768,768]{1,0:T(8,128)(2,1)} fusion(bf16[2048,768]{1,0:T(8,128)(2,1)S(1)} %add_convert_fusion.1), kind=kOutput, calls=%fused_computation.19 | convolution fusion | flops 2416508928 | bytes 4325376 | tf_op jit(solution)/shard_map/while/body/eval_jaxpr/dot_general | solution.py:34
  156.8 7.9 %multiply_convert_fusion = bf16[2048,768]{1,0:T(8,128)(2,1)} fusion(bf16[2048,768]{1,0:T(8,128)(2,1)S(1)} %add_convert_fusion.1, bf16[768,768]{1,0:T(8,128)(2,1)} %convolution_convert_fusion.2), kind=kOutput, calls=%fused_computation.11 | convolution fusion | flops 3335847936 | bytes 7471104 | tf_op jit(solution)/shard_map/while/body/eval_jaxpr/dot_general | solution.py:41
  164.7 4.0 %all-to-all-start.1 = ((bf16[32,1,64,768]{3,2,1,0:T(8,128)(2,1)}), bf16[32,1,64,768]{3,2,1,0:T(8,128)(2,1)S(1)}, u32[]{:S(2)}, u32[]{:S(2)}) async-start(bf16[32,1,64,768]{3,2,1,0:T(8,128)(2,1)} %bitcast.52), calls=%async_computation.1 | async-start | bytes 6291456 | tf_op jit(solution)/shard_map/all_to_all | solution.py:82
  168.7 72.1 %all-to-all-done.1 = bf16[32,1,64,768]{3,2,1,0:T(8,128)(2,1)S(1)} async-done(((bf16[32,1,64,768]{3,2,1,0:T(8,128)(2,1)}), bf16[32,1,64,768]{3,2,1,0:T(8,128)(2,1)S(1)}, u32[]{:S(2)}, u32[]{:S(2)}) %all-to-all-start.1) | async-done | bytes 3145760 | tf_op jit(solution)/shard_map/all_to_all | solution.py:82
  240.8 1.8 copy.14
  242.5 1.0 convolution_convert_fusion
  243.6 2.4 copy.15
  (1 shorter events, 0.0 us)
Async XLA Ops:
  0.6 54.9 %copy-start.1 = (bf16[32,64,768]{2,1,0:T(8,128)(2,1)S(1)}, bf16[32,64,768]{2,1,0:T(8,128)(2,1)}, u32[]{:S(2)}) copy-start(bf16[32,64,768]{2,1,0:T(8,128)(2,1)} %param.4) | copy-start | bytes 9437188
  0.6 54.7 %copy-start.3 = (s32[1,32]{1,0:T(1,128)S(1)}, s32[1,32]{1,0:T(1,128)}, u32[]{:S(2)}) copy-start(s32[1,32]{1,0:T(1,128)} %param.5) | copy-start | bytes 388
  58.6 1.8 copy-start
  141.7 3.7 %copy-start.2 = (bf16[32,1,64,768]{3,2,0,1:T(8,128)(2,1)}, bf16[32,1,64,768]{3,2,0,1:T(8,128)(2,1)S(1)}, u32[]{:S(2)}) copy-start(bf16[32,1,64,768]{3,2,0,1:T(8,128)(2,1)S(1)} %fusion.4) | copy-start | bytes 9437188
  164.7 76.1 %all-to-all-start.1 = ((bf16[32,1,64,768]{3,2,1,0:T(8,128)(2,1)}), bf16[32,1,64,768]{3,2,1,0:T(8,128)(2,1)S(1)}, u32[]{:S(2)}, u32[]{:S(2)}) async-start(bf16[32,1,64,768]{3,2,1,0:T(8,128)(2,1)} %bitcast.52), calls=%async_computation.1 | async-start | bytes 6291456 | tf_op jit(solution)/shard_map/all_to_all | solution.py:82
where the time goes:
time: 247 us
  blocking collectives  126 us (51%)
  waiting for transfers between devices  72.1 us (29%)
  matrix products  24.9 us (10%)
  other arithmetic  10.5 us (4%)
  local copies, waits for them, and re-layouts  6.63 us (3%)
  starting transfers between devices  4.04 us (2%)
  between operations  3.27 us (1%)
    all_to_all x1, blocking collectives, local(): lax.all_to_all(outgoing, ROW, split_axis=0, concat_axis=0, tiled=True)  75.9 us
    all_to_all x1, waiting for transfers between devices, local(): lax.all_to_all(owned, ROW, split_axis=0, concat_axis=0, tiled=True)  72.1 us
    psum x5, blocking collectives, by_axis(): return functools.reduce(lax.psum, axes, x)  49.7 us
    dot_general x2, matrix products, newton_schulz(): product = jnp.dot(iterate, poly, preferred_element_type=jnp.float32)  15.5 us
    dot_general x2, matrix products, newton_schulz(): lax.dot_general(iterate, iterate, (((0,), (0,)), ((), ())), preferred_ele...  7.4 us
    unnamed x12, local copies, waits for them, and re-layouts  6.63 us
  transfers between devices with their start and end apart: 1, of which 1 were waited for; matrix products, arithmetic and copies ran while one was open for 0% of the time, Pallas kernels for 0%

commit v1 on v0

v1 whole, which is shorter than its diff:
```python
import functools
import math

import jax
import jax.numpy as jnp
from jax import lax
from jax.experimental import pallas as pl
from jax.experimental.pallas import tpu as pltpu
from jax.sharding import Mesh
from jax.sharding import PartitionSpec as P

D = 2048
FF = 768
AXES = ("zh", "x", "y", "far", "near", "core")
SIZES = (2, 4, 4, 2, 2, 2)
EXPERT = ("zh", "x")
ROW = ("y", "far", "near", "core")
HALF = ("y", "near", "core")
HALF_SIZE = 16

quintic_one = 3.4445
quintic_two = -4.775
quintic_three = 2.0315
momentum_beta = 0.95
clip_rms = 0.25

B = 128
NB = FF // B
OFF = [(i, j) for i in range(NB) for j in range(i + 1, NB)]
PAIRS = [(i, i + 1) for i in range(0, NB, 2)]
TAIL = (len(OFF) + len(PAIRS)) * B
PACKED = TAIL + 16
f32 = jnp.float32
bf16 = jnp.bfloat16
VMEM = pl.BlockSpec(memory_space=pltpu.VMEM)


def square_kernel(g_ref, out_ref, acc):
    step = pl.program_id(0)
    values = g_ref[...].astype(f32).reshape(-1, 8, FF)
    part = jnp.sum(values * values, axis=0)

    @pl.when(step == 0)
    def _():
        acc[...] = part

    @pl.when(step > 0)
    def _():
        acc[...] += part

    @pl.when(step == pl.num_programs(0) - 1)
    def _():
        total = acc[:, 0:B]
        for j in range(1, NB):
            total = total + acc[:, j * B : (j + 1) * B]
        out_ref[...] = jnp.sum(total, axis=0, keepdims=True)


def local_squares(gradient):
    count = gradient.shape[0]
    return pl.pallas_call(
        square_kernel,
        grid=(4,),
        in_specs=[pl.BlockSpec((count // 4,) + gradient.shape[1:], lambda i: (i, 0, 0))],
        out_specs=pl.BlockSpec((1, B), lambda i: (0, 0)),
        out_shape=jax.ShapeDtypeStruct((1, B), f32),
        scratch_shapes=[pltpu.VMEM((8, FF), f32)],
        name="local_squares",
    )(gradient)


def rows_cols():
    return (
        lax.broadcasted_iota(jnp.int32, (B, B), 0),
        lax.broadcasted_iota(jnp.int32, (B, B), 1),
    )


def gram_kernel(m_ref, gram_ref, packed_ref):
    rows, cols = rows_cols()
    for i in range(3):
        lo = i * 256
        gram_ref[lo : lo + 256, lo:] = lax.dot_general(
            m_ref[:, lo : lo + 256], m_ref[:, lo:], (((0,), (0,)), ((), ())), preferred_element_type=f32
        )

    def block(i, j):
        return gram_ref[i * B : (i + 1) * B, j * B : (j + 1) * B]

    for k, (i, j) in enumerate(OFF):
        packed_ref[k * B : (k + 1) * B, :] = block(i, j).astype(bf16)
    diagonals = []
    squares = None
    for k, (i, j) in enumerate(PAIRS):
        first, second = block(i, i), block(j, j)
        lo = (len(OFF) + k) * B
        packed_ref[lo : lo + B, :] = jnp.where(rows <= cols, first, second).astype(bf16)
        diagonal = jnp.sum(jnp.where(rows == cols, second, 0.0), axis=0, keepdims=True)
        both = jnp.sum(jnp.where(rows == cols, first, 0.0), axis=0, keepdims=True) + diagonal
        diagonals.append(diagonal)
        squares = both if squares is None else squares + both
    high = squares.astype(bf16).astype(f32)
    middle = (squares - high).astype(bf16).astype(f32)
    low = squares - high - middle
    tail_rows = diagonals + [high, middle, low]
    place = lax.broadcasted_iota(jnp.int32, (16, B), 0)
    tail = jnp.zeros((16, B), f32)
    for r, row in enumerate(tail_rows):
        tail = jnp.where(place == r, jnp.broadcast_to(row, (16, B)), tail)
    packed_ref[TAIL:, :] = tail.astype(bf16)


def partial_gram(part):
    return pl.pallas_call(
        gram_kernel,
        in_specs=[VMEM],
        out_specs=[VMEM, VMEM],
        out_shape=[
            jax.ShapeDtypeStruct((FF, FF), f32),
            jax.ShapeDtypeStruct((PACKED, B), bf16),
        ],
        name="partial_gram",
        cost_estimate=pl.CostEstimate(flops=2 * part.shape[0] * FF * FF, bytes_accessed=5_000_000, transcendentals=0),
    )(part)


def update_kernel(m_ref, own_ref, packed_ref, u_ref, fro_ref, gf, gb, pb, g1b, p1b, qb):
    rows, cols = rows_cols()
    tail = packed_ref[TAIL:, :].astype(f32)
    squares = tail[3:4, :] + tail[4:5, :] + tail[5:6, :]
    for i in range(NB):
        own = own_ref[i * B : (i + 1) * B, i * B : (i + 1) * B]
        squares = squares + jnp.sum(jnp.where(rows == cols, own, 0.0), axis=0, keepdims=True)
    frobenius = jnp.sqrt(jnp.sum(squares, axis=1, keepdims=True))
    fro_ref[...] = jnp.broadcast_to(frobenius, (1, B))
    scale = 1.0 / (frobenius + 1e-07)
    scale2 = scale * scale

    def put(i, j, value):
        gf[i * B : (i + 1) * B, j * B : (j + 1) * B] = value
        gb[i * B : (i + 1) * B, j * B : (j + 1) * B] = value.astype(bf16)

    def own_block(i, j):
        return own_ref[i * B : (i + 1) * B, j * B : (j + 1) * B]

    for k, (i, j) in enumerate(OFF):
        value = (own_block(i, j) + packed_ref[k * B : (k + 1) * B, :].astype(f32)) * scale2
        put(i, j, value)
        put(j, i, value.T)
    for k, (i, j) in enumerate(PAIRS):
        lo = (len(OFF) + k) * B
        merged = packed_ref[lo : lo + B, :].astype(f32)
        turned = merged.T
        first = jnp.where(rows <= cols, merged, turned)
        second = jnp.where(rows > cols, merged, turned)
        second = jnp.where(rows == cols, jnp.broadcast_to(tail[k : k + 1, :], (B, B)), second)
        put(i, i, (own_block(i, i) + first) * scale2)
        put(j, j, (own_block(j, j) + second) * scale2)

    a, b, c = quintic_one, quintic_two, quintic_three
    strips = [slice(i * 256, (i + 1) * 256) for i in range(3)]
    for s in strips:
        square = jnp.dot(gb[s, :], gb[...], preferred_element_type=f32)
        pb[s, :] = (b * gf[s, :] + c * square).astype(bf16)
    for s in strips:
        gp = jnp.dot(gb[s, :], pb[...], preferred_element_type=f32)
        pgp = jnp.dot(gp.astype(bf16), pb[...], preferred_element_type=f32)
        g1b[s, :] = (a * a * gf[s, :] + 2.0 * a * gp + pgp).astype(bf16)
    for s in strips:
        square = jnp.dot(g1b[s, :], g1b[...], preferred_element_type=f32)
        p1b[s, :] = (b * g1b[s, :].astype(f32) + c * square).astype(bf16)
    for s in strips:
        product = jnp.dot(pb[s, :], p1b[...], preferred_element_type=f32)
        qb[s, :] = (a * (pb[s, :].astype(f32) + p1b[s, :].astype(f32)) + product).astype(bf16)
    last = scale * math.sqrt(D)
    for r in range(m_ref.shape[0] // 256):
        s = slice(r * 256, (r + 1) * 256)
        product = jnp.dot(m_ref[s, :], qb[...], preferred_element_type=f32)
        u_ref[s, :] = ((a * a * m_ref[s, :].astype(f32) + product) * last).astype(bf16)


def orthogonal_rows(part, own, packed):
    square = pltpu.VMEM((FF, FF), bf16)
    return pl.pallas_call(
        update_kernel,
        in_specs=[VMEM, VMEM, VMEM],
        out_specs=[VMEM, VMEM],
        out_shape=[
            jax.ShapeDtypeStruct(part.shape, bf16),
            jax.ShapeDtypeStruct((1, B), f32),
        ],
        scratch_shapes=[pltpu.VMEM((FF, FF), f32), square, square, square, square, square],
        name="orthogonal_rows",
        cost_estimate=pl.CostEstimate(
            flops=10 * FF**3 + 2 * part.shape[0] * FF * FF, bytes_accessed=6_000_000, transcendentals=0
        ),
    )(part, own, packed)


def swap(x, axis):
    return lax.ppermute(x, axis, [(0, 1), (1, 0)])


def local(momentum, gradient, owners):
    matrix_count = momentum.shape[0]
    row_count = momentum.shape[1]
    half = matrix_count // 2

    squares = local_squares(gradient)
    everyone = lax.axis_size(AXES)
    gathered = lax.all_to_all(
        jnp.broadcast_to(squares[None], (everyone, 1, B)), AXES, 0, 0, tiled=True
    )
    entry_count = float(everyone * gradient.size)
    factor = jnp.minimum(f32(1.0), clip_rms / jnp.sqrt(jnp.sum(gathered) / entry_count + 1e-06))

    def step(m, g):
        return (momentum_beta * m.astype(f32) + factor * g.astype(f32)).astype(bf16)

    parts = [step(momentum[i * half : (i + 1) * half], gradient[i * half : (i + 1) * half]) for i in range(2)]
    new_momentum = step(momentum, gradient)

    def gather(part):
        rows = lax.all_to_all(part, HALF, 0, 0, tiled=True)
        return rows.reshape(HALF_SIZE * row_count, FF)

    def scatter(update):
        return lax.all_to_all(update.reshape(HALF_SIZE, row_count, FF), HALF, 0, 0, tiled=True)

    rows = [gather(part) for part in parts]
    grams = [partial_gram(r) for r in rows]
    others = [swap(packed, "far") for _, packed in grams]
    others[0], sent = lax.optimization_barrier((others[0], grams[1][1]))
    first, first_norm = orthogonal_rows(rows[0], grams[0][0], others[0])
    second, second_norm = orthogonal_rows(rows[1], grams[1][0], others[1])
    froes = [first_norm, second_norm]
    updates = [scatter(first), scatter(second)]

    lanes = lax.broadcasted_iota(jnp.int32, (HALF_SIZE, B), 1)
    place = lax.broadcasted_iota(jnp.int32, (HALF_SIZE, B), 0)
    both = jnp.where(lanes == 0, froes[0], jnp.where(lanes == 1, froes[1], 0.0))
    norms = jnp.where(place == lax.axis_index(HALF), both, 0.0)
    norms = norms + swap(norms, "core")
    norms = norms + swap(norms, "near")
    norms = norms + lax.ppermute(norms, "y", [(i, i ^ 1) for i in range(4)])
    norms = norms + lax.ppermute(norms, "y", [(i, i ^ 2) for i in range(4)])
    norms = norms[:, :2].T.reshape(matrix_count)
    mine = owners[0] == lax.axis_index(ROW)
    scale = jnp.sum(jnp.where(mine, norms, 0.0)) / math.sqrt(D * FF)
    return (new_momentum, jnp.concatenate(updates, axis=0), scale.reshape(1, 1))


def solution(mesh):
    torus = Mesh(mesh.devices.reshape(SIZES), AXES)
    in_specs = (P(EXPERT, ROW, None), P(EXPERT, ROW, None), P(EXPERT, None))
    out_specs = (P(EXPERT, ROW, None), P(EXPERT, ROW, None), P(EXPERT, ROW))
    return jax.shard_map(local, mesh=torus, in_specs=in_specs, out_specs=out_specs, check_vma=False)
```

time: 247 us -> 209 us (0.85)
  blocking collectives: 126 us -> 53.5 us
  Pallas kernels: 0 us -> 31.6 us
  matrix products: 24.9 us -> 0 us
  starting transfers between devices: 4.04 us -> 21.6 us
  waiting for transfers between devices: 72.1 us -> 82.8 us
  local copies, waits for them, and re-layouts: 6.63 us -> 0.83 us
  other arithmetic: 10.5 us -> 14.5 us
    ppermute x0 -> x6, waiting for transfers between devices: none -> 53.6 us  [the longest x4 51 us: swap(): return lax.ppermute(x, axis, [(0, 1), (1, 0)])]
    psum x5 -> x0, blocking collectives: 49.7 us -> none  [by_axis(): return functools.reduce(lax.psum, axes, x)]
    all_to_all x1 -> x3, waiting for transfers between devices: 72.1 us -> 29.2 us  [the longest x1 29.2 us: gather(): rows = lax.all_to_all(part, HALF, 0, 0, tiled=True)]
    pallas_call x0 -> x5, Pallas kernels: none -> 31.6 us  [the longest x2 20.2 us: orthogonal_rows(): pl.pallas_call(update_kernel, in_specs=[VMEM, VMEM, VMEM], out_specs=[VME...]
    dot_general x6 -> x0, matrix products: 24.9 us -> none  [the longest x2 15.5 us: newton_schulz(): product = jnp.dot(iterate, poly, preferred_element_type=jnp.float32)]
    all_to_all x1 -> x2, blocking collectives: 75.9 us -> 53.5 us  [the longest x1 28.2 us: local(): lax.all_to_all(jnp.broadcast_to(squares[None], (everyone, 1, B)), AXES, 0...]
    all_to_all x1 -> x3, starting transfers between devices: 4.04 us -> 16.2 us  [the longest x2 10.9 us: scatter(): lax.all_to_all(update.reshape(HALF_SIZE, row_count, FF), HALF, 0, 0, tile...]
    unnamed x12 -> x8, local copies, waits for them, and re-layouts: 6.63 us -> 0.02 us
  transfers between devices with their start and end apart: 1 -> 9, of which waited for: 1 -> 5; matrix products, arithmetic and copies ran while one was open for 0% -> 3% of each run, Pallas kernels for 0% -> 9%
where the time goes in v1:
time: 209 us; the launch traced here: 208 us
  waiting for transfers between devices  82.8 us (40%)
  blocking collectives  53.5 us (26%)
  Pallas kernels  31.6 us (15%)
  starting transfers between devices  21.6 us (10%)
  other arithmetic  14.5 us (7%)
  between operations  3.22 us (2%)
    ppermute x4, waiting for transfers between devices, swap(): return lax.ppermute(x, axis, [(0, 1), (1, 0)])  51 us
    all_to_all x1, waiting for transfers between devices, gather(): rows = lax.all_to_all(part, HALF, 0, 0, tiled=True)  29.2 us
    all_to_all x1, blocking collectives, local(): lax.all_to_all(jnp.broadcast_to(squares[None], (everyone, 1, B)), AXES, 0...  28.2 us
    all_to_all x1, blocking collectives, gather(): rows = lax.all_to_all(part, HALF, 0, 0, tiled=True)  25.3 us
    pallas_call x2, Pallas kernels, orthogonal_rows(): pl.pallas_call(update_kernel, in_specs=[VMEM, VMEM, VMEM], out_specs=[VME...  20.2 us
    all_to_all x2, starting transfers between devices, scatter(): lax.all_to_all(update.reshape(HALF_SIZE, row_count, FF), HALF, 0, 0, tile...  10.9 us
    convert_element_type x2, other arithmetic, step(): return (momentum_beta * m.astype(f32) + factor * g.astype(f32)).astype(bf16)  9 us
    pallas_call x2, Pallas kernels, partial_gram(): pl.pallas_call(gram_kernel, in_specs=[VMEM], out_specs=[VMEM, VMEM], out_...  8.03 us
  transfers between devices with their start and end apart: 9, of which 5 were waited for; matrix products, arithmetic and copies ran while one was open for 3% of the time, Pallas kernels for 9%

profile of v1, /device:TPU:1, one launch (start us, length us, event | category | flops | bytes accessed | tf_op | source)
XLA Modules:
  0.0 208.1 jit_solution(4895237465501803979)
XLA Ops:
  0.6 0.0 copy-start
  0.6 3.4 %local_squares.1 = f32[1,128]{1,0:T(1,128)} custom-call(bf16[32,64,768]{2,1,0:T(8,128)(2,1)} %g_ref.1), custom_call_target="tpu_custom_call" | custom-call | tf_op jit(solution)/shard_map/local_squares/pallas_call | solution.py:61
  4.0 0.7 broadcast_in_dim.39
  4.7 28.2 %all_to_all.25 = f32[256,1,128]{2,1,0:T(1,128)S(1)} all-to-all(f32[256,1,128]{2,1,0:T(1,128)S(1)} %broadcast_in_dim.39), channel_id=1, replica_groups=mesh['zh'=2,'x'=4,'y'=4,'far'=2,'near'=2,'core'=2] {'zh','x','y','far','..., dimensions={0} | all-to-all | bytes 262144 | tf_op jit(solution)/shard_map/all_to_all | solution.py:211
  33.0 0.6 reduce_sum.18
  34.3 0.0 copy-done
  34.3 4.2 %add_convert_fusion.2 = (bf16[16,64,768]{2,1,0:T(8,128)(2,1)S(1)}, bf16[16,64,768]{2,1,0:T(8,128)(2,1)}) fusion(bf16[32,64,768]{2,1,0:T(8,128)(2,1)S(1)} %copy-done, f32[]{:T(128)S(6)} %min_shard_map.3, bf16[32,64,768]{2,1,0:T(8,128)(2,1)} %param.3), kind=kLoop, calls=%fused_computation.3 | loop fusion | flops 9437184 | bytes 9437188 | tf_op jit(solution)/shard_map/convert_element_type | solution.py:218
  38.5 25.3 %all_to_all.26 = bf16[16,64,768]{2,1,0:T(8,128)(2,1)} all-to-all(bf16[16,64,768]{2,1,0:T(8,128)(2,1)S(1)} %get-tuple-element.21), channel_id=1, replica_groups=mesh['zh'=2,'x'=4,'y'=4,'far'=2,'near'=2,'core'=2] {'y','near','core'}, dimensions={0} | all-to-all | bytes 3145728 | tf_op jit(solution)/shard_map/all_to_all | solution.py:224
  63.8 5.3 %all-to-all-start.2 = ((bf16[16,64,768]{2,1,0:T(8,128)(2,1)}), bf16[16,64,768]{2,1,0:T(8,128)(2,1)}, u32[]{:S(2)}, u32[]{:S(2)}) async-start(bf16[16,64,768]{2,1,0:T(8,128)(2,1)} %get-tuple-element.22), calls=%async_computation.2 | async-start | bytes 3145728 | tf_op jit(solution)/shard_map/all_to_all | solution.py:224
  69.0 4.0 %partial_gram.2 = (f32[768,768]{1,0:T(8,128)}, bf16[2320,128]{1,0:T(8,128)(2,1)}) custom-call(bf16[1024,768]{1,0:T(8,128)(2,1)} %bitcast.16), custom_call_target="tpu_custom_call" | custom-call | flops 1207959552 | bytes 5000000 | tf_op jit(solution)/shard_map/partial_gram/pallas_call | solution.py:114
  73.1 0.7 collective-permute-start
  73.7 29.2 %all-to-all-done.2 = bf16[16,64,768]{2,1,0:T(8,128)(2,1)} async-done(((bf16[16,64,768]{2,1,0:T(8,128)(2,1)}), bf16[16,64,768]{2,1,0:T(8,128)(2,1)}, u32[]{:S(2)}, u32[]{:S(2)}) %all-to-all-start.2) | async-done | bytes 1572896 | tf_op jit(solution)/shard_map/all_to_all | solution.py:224
  103.0 4.0 %partial_gram.3 = (f32[768,768]{1,0:T(8,128)}, bf16[2320,128]{1,0:T(8,128)(2,1)}) custom-call(bf16[1024,768]{1,0:T(8,128)(2,1)} %bitcast.3.m_ref), custom_call_target="tpu_custom_call" | custom-call | flops 1207959552 | bytes 5000000 | tf_op jit(solution)/shard_map/partial_gram/pallas_call | solution.py:114
  107.0 0.0 collective-permute-done.packed_ref
  107.0 10.1 %orthogonal_rows.2 = (bf16[1024,768]{1,0:T(8,128)(2,1)}, f32[1,128]{1,0:T(1,128)}) custom-call(bf16[1024,768]{1,0:T(8,128)(2,1)} %bitcast.17, f32[768,768]{1,0:T(8,128)} %get-tuple-element.12.own_ref, bf16[2320,128]{1,0:T(8,128)(2,1)} %collective-permute-done.packed_ref), custom_call_target="tpu_custom_call" | custom-call | flops 5737807872 | bytes 6000000 | tf_op jit(solution)/shard_map/orthogonal_rows/pallas_call | solution.py:184
  117.1 5.0 %all-to-all-start.3 = ((bf16[16,64,768]{2,1,0:T(8,128)(2,1)}), bf16[16,64,768]{2,1,0:T(8,128)(2,1)}, u32[]{:S(2)}, u32[]{:S(2)}) async-start(bf16[16,64,768]{2,1,0:T(8,128)(2,1)} %bitcast.18), calls=%async_computation.3 | async-start | bytes 3145728 | tf_op jit(solution)/shard_map/all_to_all | solution.py:228
  122.1 0.1 collective-permute-start.1
  122.2 31.2 %collective-permute-done.1.packed_ref = bf16[2320,128]{1,0:T(8,128)(2,1)} collective-permute-done((bf16[2320,128]{1,0:T(8,128)(2,1)}, bf16[2320,128]{1,0:T(8,128)(2,1)}, u32[]{:S(2)}, u32[]{:S(2)}) %collective-permute-start.1) | collective-permute-done | bytes 593952 | tf_op jit(solution)/shard_map/ppermute | solution.py:201
  153.5 10.1 %orthogonal_rows.3 = (bf16[1024,768]{1,0:T(8,128)(2,1)}, f32[1,128]{1,0:T(1,128)}) custom-call(bf16[1024,768]{1,0:T(8,128)(2,1)} %bitcast.3.m_ref, f32[768,768]{1,0:T(8,128)} %get-tuple-element.17.own_ref, bf16[2320,128]{1,0:T(8,128)(2,1)} %collective-permute-done.1.packed_ref), custom_call_target="tpu_custom_call" | custom-call | flops 5737807872 | bytes 6000000 | tf_op jit(solution)/shard_map/orthogonal_rows/pallas_call | solution.py:184
  163.6 0.0 copy-start.1
  163.6 0.0 copy-start.2
  163.6 0.0 copy-start.3
  163.6 0.0 all-to-all-done.3
  163.6 5.9 %all-to-all-start.4 = ((bf16[16,64,768]{2,1,0:T(8,128)(2,1)}), bf16[16,64,768]{2,1,0:T(8,128)(2,1)}, u32[]{:S(2)}, u32[]{:S(2)}) async-start(bf16[16,64,768]{2,1,0:T(8,128)(2,1)} %bitcast.15), calls=%async_computation.4 | async-start | bytes 3145728 | tf_op jit(solution)/shard_map/all_to_all | solution.py:228
  169.6 0.0 copy-done.1
  169.6 0.0 copy-done.2
  169.6 0.1 select_select_fusion
  169.7 0.2 collective-permute-start.2
  170.0 1.1 collective-permute-done.2
  171.1 0.1 fusion
  171.2 1.5 collective-permute-start.3
  172.7 18.6 %collective-permute-done.3 = f32[16,128]{0,1:T(8,128)S(1)} collective-permute-done((f32[16,128]{0,1:T(8,128)S(1)}, f32[16,128]{0,1:T(8,128)S(1)}, u32[]{:S(2)}, u32[]{:S(2)}) %collective-permute-start.3) | collective-permute-done | bytes 8224 | tf_op jit(solution)/shard_map/ppermute | solution.py:201
  191.3 0.1 fusion.4
  191.4 0.4 collective-permute-start.4
  191.9 0.0 copy-done.3
  191.9 0.1 eq.33
  192.0 2.7 %collective-permute-done.4 = f32[16,128]{0,1:T(8,128)S(1)} collective-permute-done((f32[16,128]{0,1:T(8,128)S(1)}, f32[16,128]{0,1:T(8,128)S(1)}, u32[]{:S(2)}, u32[]{:S(2)}) %collective-permute-start.4) | collective-permute-done | bytes 8224 | tf_op jit(solution)/shard_map/ppermute | solution.py:245
  194.7 2.4 %collective-permute-start.5 = (f32[16,128]{0,1:T(8,128)S(1)}, f32[16,128]{0,1:T(8,128)S(1)}, u32[]{:S(2)}, u32[]{:S(2)}) collective-permute-start(f32[16,128]{0,1:T(8,128)S(1)} %add.47), channel_id=1, source_target_pairs={{0,16},{8,24},{16,0},{24,8},{1,17},{9,25},{17,1},{25,9},{2,18},{10... | collective-permute-start | bytes 24584 | tf_op jit(solution)/shard_map/ppermute | solution.py:246
  197.1 4.8 %add_convert_fusion = bf16[32,64,768]{2,1,0:T(8,128)(2,1)} fusion(bf16[32,64,768]{2,1,0:T(8,128)(2,1)S(1)} %copy-done, bf16[32,64,768]{2,1,0:T(8,128)(2,1)} %param.3, f32[]{:T(128)S(6)} %min_shard_map.3), kind=kLoop, calls=%fused_computation | loop fusion | flops 9437184 | bytes 9437188 | tf_op jit(solution)/shard_map/convert_element_type | solution.py:218
  201.9 0.0 collective-permute-done.5
  201.9 0.6 fusion.3
  203.2 0.0 all-to-all-done.4
  203.2 3.8 %pad_maximum_fusion = bf16[32,64,768]{2,1,0:T(8,128)(2,1)} fusion(bf16[16,64,768]{2,1,0:T(8,128)(2,1)} %all-to-all-done.4, bf16[16,64,768]{2,1,0:T(8,128)(2,1)} %all-to-all-done.3), kind=kLoop, calls=%fused_computation.1 | loop fusion | flops 1572864 | bytes 6291456 | tf_op jit(solution)/shard_map/concatenate | solution.py:250
  (4 shorter events, 0.0 us)
Async XLA Ops:
  0.6 33.6 %copy-start = (bf16[32,64,768]{2,1,0:T(8,128)(2,1)S(1)}, bf16[32,64,768]{2,1,0:T(8,128)(2,1)}, u32[]{:S(2)}) copy-start(bf16[32,64,768]{2,1,0:T(8,128)(2,1)} %g_ref.1) | copy-start | bytes 9437188
  63.8 39.2 %all-to-all-start.2 = ((bf16[16,64,768]{2,1,0:T(8,128)(2,1)}), bf16[16,64,768]{2,1,0:T(8,128)(2,1)}, u32[]{:S(2)}, u32[]{:S(2)}) async-start(bf16[16,64,768]{2,1,0:T(8,128)(2,1)} %get-tuple-element.22), calls=%async_computation.2 | async-start | bytes 3145728 | tf_op jit(solution)/shard_map/all_to_all | solution.py:224
  73.1 33.9 %collective-permute-start = (bf16[2320,128]{1,0:T(8,128)(2,1)}, bf16[2320,128]{1,0:T(8,128)(2,1)}, u32[]{:S(2)}, u32[]{:S(2)}) collective-permute-start(bf16[2320,128]{1,0:T(8,128)(2,1)} %get-tuple-element.13), channel_id=1, source_target_pairs={{0,4},{4,0},{1,5},{5,1},{2,6},{6,2},{3,7},{7,3},{8,12},{12,8},{9,1... | collective-permute-start | bytes 1781768 | tf_op jit(solution)/shard_map/ppermute | solution.py:201
  117.1 46.5 %all-to-all-start.3 = ((bf16[16,64,768]{2,1,0:T(8,128)(2,1)}), bf16[16,64,768]{2,1,0:T(8,128)(2,1)}, u32[]{:S(2)}, u32[]{:S(2)}) async-start(bf16[16,64,768]{2,1,0:T(8,128)(2,1)} %bitcast.18), calls=%async_computation.3 | async-start | bytes 3145728 | tf_op jit(solution)/shard_map/all_to_all | solution.py:228
  122.1 31.4 %collective-permute-start.1 = (bf16[2320,128]{1,0:T(8,128)(2,1)}, bf16[2320,128]{1,0:T(8,128)(2,1)}, u32[]{:S(2)}, u32[]{:S(2)}) collective-permute-start(bf16[2320,128]{1,0:T(8,128)(2,1)} %get-tuple-element.14), channel_id=1, source_target_pairs={{0,4},{4,0},{1,5},{5,1},{2,6},{6,2},{3,7},{7,3},{8,12},{12,8},{9,1... | collective-permute-start | bytes 1781768 | tf_op jit(solution)/shard_map/ppermute | solution.py:201
  163.6 6.0 %copy-start.1 = (f32[1,128]{1,0:T(1,128)S(1)}, f32[1,128]{1,0:T(1,128)}, u32[]{:S(2)}) copy-start(f32[1,128]{1,0:T(1,128)} %get-tuple-element.19) | copy-start | bytes 1540
  163.6 6.0 %copy-start.2 = (f32[1,128]{1,0:T(1,128)S(1)}, f32[1,128]{1,0:T(1,128)}, u32[]{:S(2)}) copy-start(f32[1,128]{1,0:T(1,128)} %get-tuple-element.20) | copy-start | bytes 1540
  163.6 28.3 %copy-start.3 = (s32[1,32]{1,0:T(1,128)S(1)}, s32[1,32]{1,0:T(1,128)}, u32[]{:S(2)}) copy-start(s32[1,32]{1,0:T(1,128)} %param.5) | copy-start | bytes 388
  163.6 39.6 %all-to-all-start.4 = ((bf16[16,64,768]{2,1,0:T(8,128)(2,1)}), bf16[16,64,768]{2,1,0:T(8,128)(2,1)}, u32[]{:S(2)}, u32[]{:S(2)}) async-start(bf16[16,64,768]{2,1,0:T(8,128)(2,1)} %bitcast.15), calls=%async_computation.4 | async-start | bytes 3145728 | tf_op jit(solution)/shard_map/all_to_all | solution.py:228
  169.7 1.3 collective-permute-start.2
  171.2 20.1 %collective-permute-start.3 = (f32[16,128]{0,1:T(8,128)S(1)}, f32[16,128]{0,1:T(8,128)S(1)}, u32[]{:S(2)}, u32[]{:S(2)}) collective-permute-start(f32[16,128]{0,1:T(8,128)S(1)} %fusion), channel_id=1, source_target_pairs={{0,2},{2,0},{1,3},{3,1},{4,6},{6,4},{5,7},{7,5},{8,10},{10,8},{9,1... | collective-permute-start | bytes 24584 | tf_op jit(solution)/shard_map/ppermute | solution.py:201
  191.4 3.2 %collective-permute-start.4 = (f32[16,128]{0,1:T(8,128)S(1)}, f32[16,128]{0,1:T(8,128)S(1)}, u32[]{:S(2)}, u32[]{:S(2)}) collective-permute-start(f32[16,128]{0,1:T(8,128)S(1)} %fusion.4), channel_id=1, source_target_pairs={{0,8},{8,0},{16,24},{24,16},{1,9},{9,1},{17,25},{25,17},{2,10},{10... | collective-permute-start | bytes 24584 | tf_op jit(solution)/shard_map/ppermute | solution.py:245
  194.7 7.3 %collective-permute-start.5 = (f32[16,128]{0,1:T(8,128)S(1)}, f32[16,128]{0,1:T(8,128)S(1)}, u32[]{:S(2)}, u32[]{:S(2)}) collective-permute-start(f32[16,128]{0,1:T(8,128)S(1)} %add.47), channel_id=1, source_target_pairs={{0,16},{8,24},{16,0},{24,8},{1,17},{9,25},{17,1},{25,9},{2,18},{10... | collective-permute-start | bytes 24584 | tf_op jit(solution)/shard_map/ppermute | solution.py:246

commit v2 on v1

v2 whole, which is shorter than its diff:
```python
import functools
import math

import jax
import jax.numpy as jnp
from jax import lax
from jax.experimental import pallas as pl
from jax.experimental.pallas import tpu as pltpu
from jax.sharding import Mesh
from jax.sharding import PartitionSpec as P

D = 2048
FF = 768
AXES = ("zh", "x", "y", "far", "near", "core")
SIZES = (2, 4, 4, 2, 2, 2)
EXPERT = ("zh", "x")
ROW = ("y", "far", "near", "core")
HALF = ("y", "near", "core")
HALF_SIZE = 16

quintic_one = 3.4445
quintic_two = -4.775
quintic_three = 2.0315
momentum_beta = 0.95
clip_rms = 0.25

B = 128
NB = FF // B
OFF = [(i, j) for i in range(NB) for j in range(i + 1, NB)]
PAIRS = [(i, i + 1) for i in range(0, NB, 2)]
TAIL = (len(OFF) + len(PAIRS)) * B
PACKED = TAIL + 16
UPDATE_STRIPS = 4
f32 = jnp.float32
bf16 = jnp.bfloat16
VMEM = pl.BlockSpec(memory_space=pltpu.VMEM)


def square_kernel(g_ref, out_ref, acc):
    step = pl.program_id(0)

    @pl.when(step == 0)
    def _():
        acc[...] = jnp.zeros_like(acc)

    def body(k, total):
        values = g_ref[k].astype(f32)
        return total + jnp.sum((values * values).reshape(-1, 8, FF), axis=0)

    acc[...] = lax.fori_loop(0, g_ref.shape[0], body, acc[...])

    @pl.when(step == pl.num_programs(0) - 1)
    def _():
        total = acc[:, 0:B]
        for j in range(1, NB):
            total = total + acc[:, j * B : (j + 1) * B]
        total = jnp.sum(total, axis=0, keepdims=True)
        out_ref[...] = jnp.broadcast_to(total[None], out_ref.shape)


def local_squares(gradient, copies):
    count = gradient.shape[0]
    return pl.pallas_call(
        square_kernel,
        grid=(4,),
        in_specs=[pl.BlockSpec((count // 4,) + gradient.shape[1:], lambda i: (i, 0, 0))],
        out_specs=pl.BlockSpec((copies, 1, B), lambda i: (0, 0, 0)),
        out_shape=jax.ShapeDtypeStruct((copies, 1, B), f32),
        scratch_shapes=[pltpu.VMEM((8, FF), f32)],
        compiler_params=pltpu.CompilerParams(vmem_limit_bytes=16 << 20),
        name="local_squares",
    )(gradient)


def clip_factor(squares_ref, entry_count):
    total = jnp.sum(squares_ref[:, 0, :], axis=0, keepdims=True)
    total = jnp.sum(total, axis=1, keepdims=True)
    return jnp.minimum(f32(1.0), clip_rms / jnp.sqrt(total / entry_count + 1e-06))


STEP = 4


def step_kernel(entry_count, squares_ref, m_ref, g_ref, out_ref, new_ref, sems):
    factor = clip_factor(squares_ref, entry_count)
    copies = []
    for i in range(new_ref.shape[0] // STEP):
        for k in range(i * STEP, (i + 1) * STEP):
            new = momentum_beta * m_ref[k].astype(f32) + factor * g_ref[k].astype(f32)
            new_ref[k] = new.astype(bf16)
        part = pl.ds(i * STEP, STEP)
        copies.append(pltpu.make_async_copy(new_ref.at[part], out_ref.at[part], sems.at[i]))
        copies[-1].start()
    for copy in copies:
        copy.wait()


def first_step(squares, momentum, gradient, entry_count):
    shape = (momentum.shape[0] // 2,) + momentum.shape[1:]
    return pl.pallas_call(
        functools.partial(step_kernel, entry_count),
        in_specs=[VMEM, VMEM, VMEM],
        out_specs=pl.BlockSpec(memory_space=pltpu.HBM),
        out_shape=pltpu.HBM(shape, bf16),
        scratch_shapes=[pltpu.VMEM(shape, bf16), pltpu.SemaphoreType.DMA((shape[0] // STEP,))],
        compiler_params=pltpu.CompilerParams(vmem_limit_bytes=16 << 20),
        name="first_step",
    )(squares, momentum, gradient)


def whole_step_kernel(entry_count, squares_ref, m_ref, g_ref, new_ref, second_ref, sums_ref):
    step = pl.program_id(0)
    factor = clip_factor(squares_ref, entry_count)
    lanes = lax.broadcasted_iota(jnp.int32, (1, B), 1)

    @pl.when(step == 0)
    def _():
        sums_ref[...] = jnp.zeros_like(sums_ref)

    sums = sums_ref[...]
    for k in range(m_ref.shape[0]):
        new = momentum_beta * m_ref[k].astype(f32) + factor * g_ref[k].astype(f32)
        new = new.astype(bf16)
        new_ref[k] = new
        second_ref[k] = new
        values = new.astype(f32)
        part = jnp.sum((values * values).reshape(-1, 8, FF), axis=0)
        part = jnp.sum(jnp.sum(part, axis=0, keepdims=True), axis=1, keepdims=True)
        sums = sums + jnp.where(lanes == step * STEP + k, part, 0.0)
    sums_ref[...] = sums


def whole_step(squares, momentum, gradient, entry_count):
    count = momentum.shape[0]
    first = count // 2 // STEP
    block = pl.BlockSpec((STEP,) + momentum.shape[1:], lambda i: (i, 0, 0))
    second = pl.BlockSpec((STEP,) + momentum.shape[1:], lambda i: (jnp.maximum(i - first, 0), 0, 0))
    return pl.pallas_call(
        functools.partial(whole_step_kernel, entry_count),
        grid=(count // STEP,),
        in_specs=[pl.BlockSpec(squares.shape, lambda i: (0, 0, 0)), block, block],
        out_specs=[block, second, pl.BlockSpec((1, B), lambda i: (0, 0))],
        out_shape=[
            jax.ShapeDtypeStruct(momentum.shape, bf16),
            pltpu.HBM((count // 2,) + momentum.shape[1:], bf16),
            jax.ShapeDtypeStruct((1, B), f32),
        ],
        compiler_params=pltpu.CompilerParams(vmem_limit_bytes=16 << 20),
        name="whole_step",
    )(squares, momentum, gradient)


def place_kernel(offset, part_ref, *refs):
    out_ref, sems = refs[-2:]
    copies = []
    for i in range(part_ref.shape[0] // STEP):
        source = part_ref.at[pl.ds(i * STEP, STEP)]
        target = out_ref.at[pl.ds(offset + i * STEP, STEP)]
        copies.append(pltpu.make_async_copy(source, target, sems.at[i]))
        copies[-1].start()
    for copy in copies:
        copy.wait()


def place(part, offset, count, into=None):
    operands = [part] if into is None else [part, into]
    return pl.pallas_call(
        functools.partial(place_kernel, offset),
        in_specs=[pl.BlockSpec(memory_space=pl.ANY)] * len(operands),
        out_specs=pl.BlockSpec(memory_space=pltpu.HBM),
        out_shape=pltpu.HBM((count,) + part.shape[1:], bf16),
        scratch_shapes=[pltpu.SemaphoreType.DMA((part.shape[0] // STEP,))],
        input_output_aliases={} if into is None else {1: 0},
        compiler_params=pltpu.CompilerParams(vmem_limit_bytes=16 << 20),
        name="place",
    )(*operands)


def rows_cols():
    return (
        lax.broadcasted_iota(jnp.int32, (B, B), 0),
        lax.broadcasted_iota(jnp.int32, (B, B), 1),
    )


def three_parts(value):
    high = value.astype(bf16).astype(f32)
    middle = (value - high).astype(bf16).astype(f32)
    return [high, middle, value - high - middle]


def gram_kernel(m_ref, sums_ref, packed_ref, gram_ref):
    rows, cols = rows_cols()
    for i in range(3):
        lo = i * 256
        gram_ref[lo : lo + 256, lo:] = lax.dot_general(
            m_ref[:, lo : lo + 256], m_ref[:, lo:], (((0,), (0,)), ((), ())), preferred_element_type=f32
        )

    def block(i, j):
        return gram_ref[i * B : (i + 1) * B, j * B : (j + 1) * B]

    for k, (i, j) in enumerate(OFF):
        packed_ref[k * B : (k + 1) * B, :] = block(i, j).astype(bf16)
    diagonals = []
    squares = None
    for k, (i, j) in enumerate(PAIRS):
        first, second = block(i, i), block(j, j)
        lo = (len(OFF) + k) * B
        packed_ref[lo : lo + B, :] = jnp.where(rows <= cols, first, second).astype(bf16)
        diagonal = jnp.sum(jnp.where(rows == cols, second, 0.0), axis=0, keepdims=True)
        both = jnp.sum(jnp.where(rows == cols, first, 0.0), axis=0, keepdims=True) + diagonal
        diagonals.append(diagonal)
        squares = both if squares is None else squares + both
    tail_rows = diagonals + three_parts(squares) + three_parts(sums_ref[...])
    place = lax.broadcasted_iota(jnp.int32, (16, B), 0)
    tail = jnp.zeros((16, B), f32)
    for r, row in enumerate(tail_rows):
        tail = jnp.where(place == r, jnp.broadcast_to(row, (16, B)), tail)
    packed_ref[TAIL:, :] = tail.astype(bf16)


def partial_gram(part, sums):
    return pl.pallas_call(
        gram_kernel,
        in_specs=[VMEM, VMEM],
        out_specs=VMEM,
        out_shape=jax.ShapeDtypeStruct((PACKED, B), bf16),
        scratch_shapes=[pltpu.VMEM((FF, FF), f32)],
        compiler_params=pltpu.CompilerParams(vmem_limit_bytes=24 << 20),
        name="partial_gram",
        cost_estimate=pl.CostEstimate(flops=2 * part.shape[0] * FF * FF, bytes_accessed=2_000_000, transcendentals=0),
    )(part, sums)


def update_kernel(m_ref, own_ref, other_ref, out_ref, gf, gb, pb, g1b, p1b, qb, u_ref, sems):
    rows, cols = rows_cols()

    def summed(lo, size):
        return own_ref[lo : lo + size, :].astype(f32) + other_ref[lo : lo + size, :].astype(f32)

    tail = summed(TAIL, 16)
    squares = jnp.sum(tail[3:6, :], axis=0, keepdims=True)
    frobenius = jnp.sqrt(jnp.sum(squares, axis=1, keepdims=True))
    scale = 1.0 / (frobenius + 1e-07)
    scale2 = scale * scale

    def put(i, j, value):
        gf[i * B : (i + 1) * B, j * B : (j + 1) * B] = value
        gb[i * B : (i + 1) * B, j * B : (j + 1) * B] = value.astype(bf16)

    for k, (i, j) in enumerate(OFF):
        value = summed(k * B, B) * scale2
        put(i, j, value)
        put(j, i, value.T)
    for k, (i, j) in enumerate(PAIRS):
        merged = summed((len(OFF) + k) * B, B) * scale2
        turned = merged.T
        put(i, i, jnp.where(rows <= cols, merged, turned))
        second = jnp.where(rows > cols, merged, turned)
        put(j, j, jnp.where(rows == cols, jnp.broadcast_to(tail[k : k + 1, :] * scale2, (B, B)), second))

    a, b, c = quintic_one, quintic_two, quintic_three
    strips = [slice(i * 256, (i + 1) * 256) for i in range(3)]
    for s in strips:
        square = jnp.dot(gb[s, :], gb[...], preferred_element_type=f32)
        pb[s, :] = (b * gf[s, :] + c * square).astype(bf16)
    for s in strips:
        gp = jnp.dot(gb[s, :], pb[...], preferred_element_type=f32)
        pgp = jnp.dot(gp.astype(bf16), pb[...], preferred_element_type=f32)
        g1b[s, :] = (a * a * gf[s, :] + 2.0 * a * gp + pgp).astype(bf16)
    for s in strips:
        square = jnp.dot(g1b[s, :], g1b[...], preferred_element_type=f32)
        p1b[s, :] = (b * g1b[s, :].astype(f32) + c * square).astype(bf16)
    for s in strips:
        product = jnp.dot(pb[s, :], p1b[...], preferred_element_type=f32)
        qb[s, :] = (a * (pb[s, :].astype(f32) + p1b[s, :].astype(f32)) + product).astype(bf16)
    last = scale * math.sqrt(D)
    copies = []
    for r in range(UPDATE_STRIPS):
        s = pl.ds(r * 256, 256)
        product = jnp.dot(m_ref[s, :], qb[...], preferred_element_type=f32)
        u_ref[s, :] = ((a * a * m_ref[s, :].astype(f32) + product) * last).astype(bf16)
        copies.append(pltpu.make_async_copy(u_ref.at[s, :], out_ref.at[s, :], sems.at[r]))
        copies[-1].start()
    for copy in copies:
        copy.wait()


def orthogonal_rows(part, own, other):
    square = pltpu.VMEM((FF, FF), bf16)
    return pl.pallas_call(
        update_kernel,
        in_specs=[VMEM, VMEM, VMEM],
        out_specs=pl.BlockSpec(memory_space=pltpu.HBM),
        out_shape=pltpu.HBM(part.shape, bf16),
        scratch_shapes=[
            pltpu.VMEM((FF, FF), f32),
            square,
            square,
            square,
            square,
            square,
            pltpu.VMEM(part.shape, bf16),
            pltpu.SemaphoreType.DMA((UPDATE_STRIPS,)),
        ],
        compiler_params=pltpu.CompilerParams(vmem_limit_bytes=32 << 20),
        name="orthogonal_rows",
        cost_estimate=pl.CostEstimate(flops=60_000_000_000, bytes_accessed=6_000_000, transcendentals=0),
    )(part, own, other)


def swap(x, axis):
    return lax.ppermute(x, axis, [(0, 1), (1, 0)])


def local(momentum, gradient, owners):
    matrix_count = momentum.shape[0]
    row_count = momentum.shape[1]
    half = matrix_count // 2

    everyone = lax.axis_size(AXES)
    entry_count = float(everyone * gradient.size)
    squares = lax.all_to_all(local_squares(gradient, everyone), AXES, 0, 0, tiled=True)

    def gather(part):
        rows = lax.all_to_all(part, HALF, 0, 0, tiled=True)
        return rows.reshape(HALF_SIZE * row_count, FF)

    def scatter(update):
        return lax.all_to_all(update.reshape(HALF_SIZE, row_count, FF), HALF, 0, 0, tiled=True)

    first = gather(first_step(squares, momentum, gradient, entry_count))
    new_momentum, second, sums = whole_step(squares, momentum, gradient, entry_count)
    sums = sums + swap(sums, "core")
    sums = sums + swap(sums, "near")
    first, sums = lax.optimization_barrier((first, sums))
    own_first = partial_gram(first, sums)
    second, own_first = lax.optimization_barrier((second, own_first))
    other_first = swap(own_first, "far")
    rows = gather(second)
    both = own_first[TAIL + 6 : TAIL + 9].astype(f32) + other_first[TAIL + 6 : TAIL + 9].astype(f32)
    sums = jnp.sum(both, axis=0, keepdims=True)
    around = [lax.ppermute(sums, "y", [(i, (i + k) % 4) for i in range(4)]) for k in range(1, 4)]
    first = orthogonal_rows(first, own_first, other_first)
    sums = functools.reduce(jnp.add, around, sums)
    rows, first, sums = lax.optimization_barrier((rows, first, sums))
    own_second = partial_gram(rows, sums)
    other_second = swap(own_second, "far")
    first, own_second = lax.optimization_barrier((first, own_second))
    first = scatter(first)
    second = scatter(orthogonal_rows(rows, own_second, other_second))
    updates = place(first, 0, matrix_count)
    updates = place(second, half, matrix_count, updates)

    mine = owners[0] == lax.axis_index(ROW)
    norm = jnp.sqrt(jnp.sum(jnp.where(mine, sums[0, :matrix_count], 0.0)))
    return (new_momentum, updates, (norm / math.sqrt(D * FF)).reshape(1, 1))


def solution(mesh):
    torus = Mesh(mesh.devices.reshape(SIZES), AXES)
    in_specs = (P(EXPERT, ROW, None), P(EXPERT, ROW, None), P(EXPERT, None))
    out_specs = (P(EXPERT, ROW, None), P(EXPERT, ROW, None), P(EXPERT, ROW))
    return jax.shard_map(local, mesh=torus, in_specs=in_specs, out_specs=out_specs, check_vma=False)
```

time: 209 us -> 174 us (0.83)
  blocking collectives: 53.5 us -> 28.2 us
  other arithmetic: 14.5 us -> 0.64 us
  starting transfers between devices: 21.6 us -> 26.7 us
  waiting for transfers between devices: 82.8 us -> 79.6 us
  local copies, waits for them, and re-layouts: 0.83 us -> 3.78 us
    all_to_all x1 -> x2, waiting for transfers between devices: 29.2 us -> 1.72 us  [gather(): rows = lax.all_to_all(part, HALF, 0, 0, tiled=True)]
    all_to_all x2 -> x1, blocking collectives: 53.5 us -> 28.2 us  [local(): lax.all_to_all(local_squares(gradient, everyone), AXES, 0, 0, tiled=True)]
    all_to_all x2, waiting for transfers between devices: 0.01 us -> 23.1 us  [scatter(): lax.all_to_all(update.reshape(HALF_SIZE, row_count, FF), HALF, 0, 0, tile...]
    convert_element_type x2 -> x0, other arithmetic: 9 us -> none  [step(): return (momentum_beta * m.astype(f32) + factor * g.astype(f32)).astype(bf16)]
    all_to_all x1 -> x2, starting transfers between devices: 5.29 us -> 10.1 us  [gather(): rows = lax.all_to_all(part, HALF, 0, 0, tiled=True)]
    concatenate x1 -> x0, other arithmetic: 3.82 us -> none  [local(): return (new_momentum, jnp.concatenate(updates, axis=0), scale.reshape(1, 1))]
    ppermute x4, waiting for transfers between devices: 51 us -> 54.8 us  [swap(): return lax.ppermute(x, axis, [(0, 1), (1, 0)])]
    unnamed x8 -> x10, local copies, waits for them, and re-layouts: 0.02 us -> 3.78 us
  transfers between devices with their start and end apart: 9 -> 11, of which waited for: 5 -> 7; matrix products, arithmetic and copies ran while one was open for 3% -> 0% of each run, Pallas kernels for 9% -> 14%
where the time goes in v2:
time: 174 us
  waiting for transfers between devices  79.6 us (46%)
  Pallas kernels  32.3 us (19%)
  blocking collectives  28.2 us (16%)
  starting transfers between devices  26.7 us (15%)
  local copies, waits for them, and re-layouts  3.78 us (2%)
  between operations  2.58 us (1%)
    ppermute x4, waiting for transfers between devices, swap(): return lax.ppermute(x, axis, [(0, 1), (1, 0)])  54.8 us
    all_to_all x1, blocking collectives, local(): lax.all_to_all(local_squares(gradient, everyone), AXES, 0, 0, tiled=True)  28.2 us
    all_to_all x2, waiting for transfers between devices, scatter(): lax.all_to_all(update.reshape(HALF_SIZE, row_count, FF), HALF, 0, 0, tile...  23.1 us
    pallas_call x2, Pallas kernels, orthogonal_rows(): pl.pallas_call(update_kernel, in_specs=[VMEM, VMEM, VMEM], out_specs=pl.B...  17.6 us
    all_to_all x2, starting transfers between devices, scatter(): lax.all_to_all(update.reshape(HALF_SIZE, row_count, FF), HALF, 0, 0, tile...  11.2 us
    all_to_all x2, starting transfers between devices, gather(): rows = lax.all_to_all(part, HALF, 0, 0, tiled=True)  10.1 us
    pallas_call x1, Pallas kernels, whole_step(): pl.pallas_call(functools.partial(whole_step_kernel, entry_count), grid=(c...  5.97 us
    pallas_call x2, Pallas kernels, partial_gram(): pl.pallas_call(gram_kernel, in_specs=[VMEM, VMEM], out_specs=VMEM, out_sh...  4.29 us
  transfers between devices with their start and end apart: 11, of which 7 were waited for; matrix products, arithmetic and copies ran while one was open for 0% of the time, Pallas kernels for 14%

profile of v2, /device:TPU:1, one launch (start us, length us, event | category | flops | bytes accessed | tf_op | source)
XLA Modules:
  0.0 173.8 jit_solution(10063889587041406101)
XLA Ops:
  0.6 0.0 copy-start
  0.6 1.9 %copy-done = bf16[32,64,768]{2,1,0:T(8,128)(2,1)S(1)} copy-done((bf16[32,64,768]{2,1,0:T(8,128)(2,1)S(1)}, bf16[32,64,768]{2,1,0:T(8,128)(2,1)}, u32[]{:S(2)}) %copy-start) | copy-done | bytes 3145752
  2.5 0.0 copy-start.2
  2.5 0.5 local_squares.1
  3.1 28.2 %all_to_all.25.squares_ref = f32[256,1,128]{2,1,0:T(1,128)S(1)} all-to-all(f32[256,1,128]{2,1,0:T(1,128)S(1)} %local_squares.1), channel_id=1, replica_groups=mesh['zh'=2,'x'=4,'y'=4,'far'=2,'near'=2,'core'=2] {'zh','x','y','far','..., dimensions={0} | all-to-all | bytes 262144 | tf_op jit(solution)/shard_map/all_to_all | solution.py:324
  31.3 0.0 copy-done.2
  31.3 1.6 first_step.1
  32.9 0.0 copy-start.1
  32.9 5.4 %all-to-all-start.1 = ((bf16[16,64,768]{2,1,0:T(8,128)(2,1)}), bf16[16,64,768]{2,1,0:T(8,128)(2,1)}, u32[]{:S(2)}, u32[]{:S(2)}) async-start(bf16[16,64,768]{2,1,0:T(8,128)(2,1)} %first_step.1), calls=%async_computation.1 | async-start | bytes 3145728 | tf_op jit(solution)/shard_map/all_to_all | solution.py:327
  38.3 0.0 copy-done.1
  38.4 0.0 copy-start.3
  38.4 1.9 %copy-done.3 = bf16[32,64,768]{2,1,0:T(8,128)(2,1)S(1)} copy-done((bf16[32,64,768]{2,1,0:T(8,128)(2,1)S(1)}, bf16[32,64,768]{2,1,0:T(8,128)(2,1)}, u32[]{:S(2)}) %copy-start.3) | copy-done | bytes 3145752
  40.2 6.0 %whole_step.1 = (bf16[32,64,768]{2,1,0:T(8,128)(2,1)}, bf16[16,64,768]{2,1,0:T(8,128)(2,1)}, f32[1,128]{1,0:T(1,128)S(1)}) custom-call(f32[256,1,128]{2,1,0:T(1,128)S(1)} %all_to_all.25.squares_ref, bf16[32,64,768]{2,1,0:T(8,128)(2,1)S(1)} %copy-done.3, bf16[32,64,768]{2,1,0:T(8,128)(2,1)S(1)} %copy-done.1), custom_call_target="tpu_custom_call" | custom-call | tf_op jit(solution)/shard_map/whole_step/pallas_call | solution.py:138
  46.2 0.3 collective-permute-start
  46.5 0.8 collective-permute-done
  47.3 1.5 collective-permute-start.1
  48.8 9.5 %collective-permute-done.1 = f32[1,128]{1,0:T(1,128)S(1)} collective-permute-done((f32[1,128]{1,0:T(1,128)S(1)}, f32[1,128]{1,0:T(1,128)S(1)}, u32[]{:S(2)}, u32[]{:S(2)}) %collective-permute-start.1) | collective-permute-done | bytes 544 | tf_op jit(solution)/shard_map/ppermute | solution.py:314
  58.3 1.7 all-to-all-done.1
  60.0 2.4 %partial_gram.2.own_ref = bf16[2320,128]{1,0:T(8,128)(2,1)S(1)} custom-call(bf16[1024,768]{1,0:T(8,128)(2,1)} %bitcast.m_ref, f32[1,128]{1,0:T(1,128)S(1)} %add.28.sums_ref), custom_call_target="tpu_custom_call" | custom-call | flops 1207959552 | bytes 2000000 | tf_op jit(solution)/shard_map/partial_gram/pallas_call | solution.py:224
  62.5 0.8 collective-permute-start.2
  63.3 4.7 %all-to-all-start.2 = ((bf16[16,64,768]{2,1,0:T(8,128)(2,1)}), bf16[16,64,768]{2,1,0:T(8,128)(2,1)S(1)}, u32[]{:S(2)}, u32[]{:S(2)}) async-start(bf16[16,64,768]{2,1,0:T(8,128)(2,1)} %get-tuple-element.20), calls=%async_computation.2 | async-start | bytes 3145728 | tf_op jit(solution)/shard_map/all_to_all | solution.py:327
  67.9 23.1 %collective-permute-done.2.other_ref = bf16[2320,128]{1,0:T(8,128)(2,1)S(1)} collective-permute-done((bf16[2320,128]{1,0:T(8,128)(2,1)S(1)}, bf16[2320,128]{1,0:T(8,128)(2,1)S(1)}, u32[]{:S(2)}, u32[]{:S(2)}) %collective-permute-start.2) | collective-permute-done | bytes 593952 | tf_op jit(solution)/shard_map/ppermute | solution.py:314
  91.0 1.1 collective-permute-start.4
  92.1 1.7 collective-permute-start.5
  93.9 0.0 collective-permute-start.3
  93.9 8.8 %orthogonal_rows.2 = bf16[1024,768]{1,0:T(8,128)(2,1)} custom-call(bf16[1024,768]{1,0:T(8,128)(2,1)} %bitcast.m_ref, bf16[2320,128]{1,0:T(8,128)(2,1)S(1)} %partial_gram.2.own_ref, bf16[2320,128]{1,0:T(8,128)(2,1)S(1)} %collective-permute-done.2.other_ref), custom_call_target="tpu_custom_call" | custom-call | flops 60000002048 | bytes 6000000 | tf_op jit(solution)/shard_map/orthogonal_rows/pallas_call | solution.py:292
  102.7 0.0 collective-permute-done.4
  102.7 0.0 collective-permute-done.5
  102.7 0.0 collective-permute-done.3
  102.8 0.0 all-to-all-done.2
  102.8 1.9 %partial_gram.3.own_ref = bf16[2320,128]{1,0:T(8,128)(2,1)} custom-call(bf16[1024,768]{1,0:T(8,128)(2,1)S(1)} %bitcast.7, f32[1,128]{1,0:T(1,128)S(1)} %add_add_fusion.sums_ref), custom_call_target="tpu_custom_call" | custom-call | flops 1207959552 | bytes 2000000 | tf_op jit(solution)/shard_map/partial_gram/pallas_call | solution.py:224
  104.6 0.0 collective-permute-start.6
  104.6 6.7 %all-to-all-start.4 = ((bf16[16,64,768]{2,1,0:T(8,128)(2,1)}), bf16[16,64,768]{2,1,0:T(8,128)(2,1)S(1)}, u32[]{:S(2)}, u32[]{:S(2)}) async-start(bf16[16,64,768]{2,1,0:T(8,128)(2,1)} %bitcast.10), calls=%async_computation.4 | async-start | bytes 3145728 | tf_op jit(solution)/shard_map/all_to_all | solution.py:331
  111.4 21.3 %collective-permute-done.6.other_ref = bf16[2320,128]{1,0:T(8,128)(2,1)} collective-permute-done((bf16[2320,128]{1,0:T(8,128)(2,1)}, bf16[2320,128]{1,0:T(8,128)(2,1)}, u32[]{:S(2)}, u32[]{:S(2)}) %collective-permute-start.6) | collective-permute-done | bytes 593952 | tf_op jit(solution)/shard_map/ppermute | solution.py:314
  132.7 8.7 %orthogonal_rows.3 = bf16[1024,768]{1,0:T(8,128)(2,1)} custom-call(bf16[1024,768]{1,0:T(8,128)(2,1)S(1)} %bitcast.8, bf16[2320,128]{1,0:T(8,128)(2,1)} %partial_gram.3.own_ref, bf16[2320,128]{1,0:T(8,128)(2,1)} %collective-permute-done.6.other_ref), custom_call_target="tpu_custom_call" | custom-call | flops 60000002048 | bytes 6000000 | tf_op jit(solution)/shard_map/orthogonal_rows/pallas_call | solution.py:292
  141.4 4.0 %all-to-all-done.4.part_ref = bf16[16,64,768]{2,1,0:T(8,128)(2,1)S(1)} async-done(((bf16[16,64,768]{2,1,0:T(8,128)(2,1)}), bf16[16,64,768]{2,1,0:T(8,128)(2,1)S(1)}, u32[]{:S(2)}, u32[]{:S(2)}) %all-to-all-start.4) | async-done | bytes 1572896 | tf_op jit(solution)/shard_map/all_to_all | solution.py:331
  145.4 0.0 copy-start.4
  145.4 4.5 %all-to-all-start.3 = ((bf16[16,64,768]{2,1,0:T(8,128)(2,1)}), bf16[16,64,768]{2,1,0:T(8,128)(2,1)S(1)}, u32[]{:S(2)}, u32[]{:S(2)}) async-start(bf16[16,64,768]{2,1,0:T(8,128)(2,1)} %bitcast.9), calls=%async_computation.3 | async-start | bytes 3145728 | tf_op jit(solution)/shard_map/all_to_all | solution.py:331
  149.9 0.0 copy-done.4
  149.9 0.6 fusion
  151.2 1.2 place.2.refs_0_
  152.4 19.1 %all-to-all-done.3.part_ref = bf16[16,64,768]{2,1,0:T(8,128)(2,1)S(1)} async-done(((bf16[16,64,768]{2,1,0:T(8,128)(2,1)}), bf16[16,64,768]{2,1,0:T(8,128)(2,1)S(1)}, u32[]{:S(2)}, u32[]{:S(2)}) %all-to-all-start.3) | async-done | bytes 1572896 | tf_op jit(solution)/shard_map/all_to_all | solution.py:331
  171.5 1.2 place.3
  (4 shorter events, 0.0 us)
Async XLA Ops:
  0.6 1.9 %copy-start = (bf16[32,64,768]{2,1,0:T(8,128)(2,1)S(1)}, bf16[32,64,768]{2,1,0:T(8,128)(2,1)}, u32[]{:S(2)}) copy-start(bf16[32,64,768]{2,1,0:T(8,128)(2,1)} %g_ref.5) | copy-start | bytes 9437188
  2.5 28.8 %copy-start.2 = (bf16[32,64,768]{2,1,0:T(8,128)(2,1)S(1)}, bf16[32,64,768]{2,1,0:T(8,128)(2,1)}, u32[]{:S(2)}) copy-start(bf16[32,64,768]{2,1,0:T(8,128)(2,1)} %m_ref.3) | copy-start | bytes 9437188
  32.9 5.5 %copy-start.1 = (bf16[32,64,768]{2,1,0:T(8,128)(2,1)S(1)}, bf16[32,64,768]{2,1,0:T(8,128)(2,1)}, u32[]{:S(2)}) copy-start(bf16[32,64,768]{2,1,0:T(8,128)(2,1)} %g_ref.5) | copy-start | bytes 9437188
  32.9 27.1 %all-to-all-start.1 = ((bf16[16,64,768]{2,1,0:T(8,128)(2,1)}), bf16[16,64,768]{2,1,0:T(8,128)(2,1)}, u32[]{:S(2)}, u32[]{:S(2)}) async-start(bf16[16,64,768]{2,1,0:T(8,128)(2,1)} %first_step.1), calls=%async_computation.1 | async-start | bytes 3145728 | tf_op jit(solution)/shard_map/all_to_all | solution.py:327
  38.4 1.9 %copy-start.3 = (bf16[32,64,768]{2,1,0:T(8,128)(2,1)S(1)}, bf16[32,64,768]{2,1,0:T(8,128)(2,1)}, u32[]{:S(2)}) copy-start(bf16[32,64,768]{2,1,0:T(8,128)(2,1)} %m_ref.3) | copy-start | bytes 9437188
  46.2 1.1 collective-permute-start
  47.3 11.0 %collective-permute-start.1 = (f32[1,128]{1,0:T(1,128)S(1)}, f32[1,128]{1,0:T(1,128)S(1)}, u32[]{:S(2)}, u32[]{:S(2)}) collective-permute-start(f32[1,128]{1,0:T(1,128)S(1)} %add.27), channel_id=1, source_target_pairs={{0,2},{2,0},{1,3},{3,1},{4,6},{6,4},{5,7},{7,5},{8,10},{10,8},{9,1... | collective-permute-start | bytes 1544 | tf_op jit(solution)/shard_map/ppermute | solution.py:314
  62.5 28.5 %collective-permute-start.2 = (bf16[2320,128]{1,0:T(8,128)(2,1)S(1)}, bf16[2320,128]{1,0:T(8,128)(2,1)S(1)}, u32[]{:S(2)}, u32[]{:S(2)}) collective-permute-start(bf16[2320,128]{1,0:T(8,128)(2,1)S(1)} %partial_gram.2.own_ref), channel_id=1, source_target_pairs={{0,4},{4,0},{1,5},{5,1},{2,6},{6,2},{3,7},{7,3},{8,12},{12,8},{9,1... | collective-permute-start | bytes 1781768 | tf_op jit(solution)/shard_map/ppermute | solution.py:314
  63.3 39.5 %all-to-all-start.2 = ((bf16[16,64,768]{2,1,0:T(8,128)(2,1)}), bf16[16,64,768]{2,1,0:T(8,128)(2,1)S(1)}, u32[]{:S(2)}, u32[]{:S(2)}) async-start(bf16[16,64,768]{2,1,0:T(8,128)(2,1)} %get-tuple-element.20), calls=%async_computation.2 | async-start | bytes 3145728 | tf_op jit(solution)/shard_map/all_to_all | solution.py:327
  91.0 11.7 %collective-permute-start.4 = (f32[1,128]{1,0:T(1,128)S(1)}, f32[1,128]{1,0:T(1,128)S(1)}, u32[]{:S(2)}, u32[]{:S(2)}) collective-permute-start(f32[1,128]{1,0:T(1,128)S(1)} %bitcast.11), channel_id=1, source_target_pairs={{0,16},{8,24},{16,0},{24,8},{1,17},{9,25},{17,1},{25,9},{2,18},{10... | collective-permute-start | bytes 1544 | tf_op jit(solution)/shard_map/ppermute | solution.py:344
  92.1 10.6 %collective-permute-start.5 = (f32[1,128]{1,0:T(1,128)S(1)}, f32[1,128]{1,0:T(1,128)S(1)}, u32[]{:S(2)}, u32[]{:S(2)}) collective-permute-start(f32[1,128]{1,0:T(1,128)S(1)} %bitcast.12), channel_id=1, source_target_pairs={{0,24},{8,0},{16,8},{24,16},{1,25},{9,1},{17,9},{25,17},{2,26},{10... | collective-permute-start | bytes 1544 | tf_op jit(solution)/shard_map/ppermute | solution.py:344
  93.9 8.9 %collective-permute-start.3 = (f32[1,128]{1,0:T(1,128)S(1)}, f32[1,128]{1,0:T(1,128)S(1)}, u32[]{:S(2)}, u32[]{:S(2)}) collective-permute-start(f32[1,128]{1,0:T(1,128)S(1)} %bitcast.13), channel_id=1, source_target_pairs={{0,8},{8,16},{16,24},{24,0},{1,9},{9,17},{17,25},{25,1},{2,10},{10... | collective-permute-start | bytes 1544 | tf_op jit(solution)/shard_map/ppermute | solution.py:344
  104.6 28.1 %collective-permute-start.6 = (bf16[2320,128]{1,0:T(8,128)(2,1)}, bf16[2320,128]{1,0:T(8,128)(2,1)}, u32[]{:S(2)}, u32[]{:S(2)}) collective-permute-start(bf16[2320,128]{1,0:T(8,128)(2,1)} %partial_gram.3.own_ref), channel_id=1, source_target_pairs={{0,4},{4,0},{1,5},{5,1},{2,6},{6,2},{3,7},{7,3},{8,12},{12,8},{9,1... | collective-permute-start | bytes 1781768 | tf_op jit(solution)/shard_map/ppermute | solution.py:314
  104.6 40.8 %all-to-all-start.4 = ((bf16[16,64,768]{2,1,0:T(8,128)(2,1)}), bf16[16,64,768]{2,1,0:T(8,128)(2,1)S(1)}, u32[]{:S(2)}, u32[]{:S(2)}) async-start(bf16[16,64,768]{2,1,0:T(8,128)(2,1)} %bitcast.10), calls=%async_computation.4 | async-start | bytes 3145728 | tf_op jit(solution)/shard_map/all_to_all | solution.py:331
  145.4 4.5 %copy-start.4 = (s32[1,32]{1,0:T(1,128)S(1)}, s32[1,32]{1,0:T(1,128)}, u32[]{:S(2)}) copy-start(s32[1,32]{1,0:T(1,128)} %param.5) | copy-start | bytes 388
  145.4 26.1 %all-to-all-start.3 = ((bf16[16,64,768]{2,1,0:T(8,128)(2,1)}), bf16[16,64,768]{2,1,0:T(8,128)(2,1)S(1)}, u32[]{:S(2)}, u32[]{:S(2)}) async-start(bf16[16,64,768]{2,1,0:T(8,128)(2,1)} %bitcast.9), calls=%async_computation.3 | async-start | bytes 3145728 | tf_op jit(solution)/shard_map/all_to_all | solution.py:331

commit v3 on v2

--- a/solution.py
+++ b/solution.py
@@ -341,16 +341,17 @@
     rows = gather(second)
     both = own_first[TAIL + 6 : TAIL + 9].astype(f32) + other_first[TAIL + 6 : TAIL + 9].astype(f32)
     sums = jnp.sum(both, axis=0, keepdims=True)
-    around = [lax.ppermute(sums, "y", [(i, (i + k) % 4) for i in range(4)]) for k in range(1, 4)]
     first = orthogonal_rows(first, own_first, other_first)
-    sums = functools.reduce(jnp.add, around, sums)
-    rows, first, sums = lax.optimization_barrier((rows, first, sums))
+    rows, first = lax.optimization_barrier((rows, first))
     own_second = partial_gram(rows, sums)
     other_second = swap(own_second, "far")
     first, own_second = lax.optimization_barrier((first, own_second))
     first = scatter(first)
     second = scatter(orthogonal_rows(rows, own_second, other_second))
     updates = place(first, 0, matrix_count)
+    updates, sums = lax.optimization_barrier((updates, sums))
+    around = [lax.ppermute(sums, "y", [(i, (i + k) % 4) for i in range(4)]) for k in range(1, 4)]
+    sums = functools.reduce(jnp.add, around, sums)
     updates = place(second, half, matrix_count, updates)
 
     mine = owners[0] == lax.axis_index(ROW)

time: 174 us -> 171 us (0.983)
  waiting for transfers between devices: 79.6 us -> 76.7 us
    all_to_all x2, waiting for transfers between devices: 23.1 us -> 4.08 us  [scatter(): lax.all_to_all(update.reshape(HALF_SIZE, row_count, FF), HALF, 0, 0, tile...]
    ppermute x3, waiting for transfers between devices: 0.01 us -> 13 us  [local(): lax.ppermute(sums, 'y', [(i, (i + k) % 4) for i in range(4)])]
    all_to_all x2, starting transfers between devices: 11.2 us -> 8.87 us  [scatter(): lax.all_to_all(update.reshape(HALF_SIZE, row_count, FF), HALF, 0, 0, tile...]
    ppermute x3, starting transfers between devices: 2.87 us -> 5.09 us  [local(): lax.ppermute(sums, 'y', [(i, (i + k) % 4) for i in range(4)])]
    all_to_all x2, waiting for transfers between devices: 1.72 us -> 3.9 us  [gather(): rows = lax.all_to_all(part, HALF, 0, 0, tiled=True)]
  transfers between devices with their start and end apart: 11 -> 11, of which waited for: 7 -> 11; matrix products, arithmetic and copies ran while one was open for 0% -> 0% of each run, Pallas kernels for 14% -> 14%
where the time goes in v3:
time: 171 us
  waiting for transfers between devices  76.7 us (45%)
  Pallas kernels  32.3 us (19%)
  blocking collectives  28.2 us (16%)
  starting transfers between devices  26.6 us (16%)
  local copies, waits for them, and re-layouts  3.78 us (2%)
  between operations  2.55 us (1%)
    ppermute x4, waiting for transfers between devices, swap(): return lax.ppermute(x, axis, [(0, 1), (1, 0)])  55.7 us
    all_to_all x1, blocking collectives, local(): lax.all_to_all(local_squares(gradient, everyone), AXES, 0, 0, tiled=True)  28.2 us
    pallas_call x2, Pallas kernels, orthogonal_rows(): pl.pallas_call(update_kernel, in_specs=[VMEM, VMEM, VMEM], out_specs=pl.B...  17.6 us
    ppermute x3, waiting for transfers between devices, local(): lax.ppermute(sums, 'y', [(i, (i + k) % 4) for i in range(4)])  13 us
    all_to_all x2, starting transfers between devices, gather(): rows = lax.all_to_all(part, HALF, 0, 0, tiled=True)  10.1 us
    all_to_all x2, starting transfers between devices, scatter(): lax.all_to_all(update.reshape(HALF_SIZE, row_count, FF), HALF, 0, 0, tile...  8.87 us
    pallas_call x1, Pallas kernels, whole_step(): pl.pallas_call(functools.partial(whole_step_kernel, entry_count), grid=(c...  5.97 us
    ppermute x3, starting transfers between devices, local(): lax.ppermute(sums, 'y', [(i, (i + k) % 4) for i in range(4)])  5.09 us
  transfers between devices with their start and end apart: 11, of which 11 were waited for; matrix products, arithmetic and copies ran while one was open for 0% of the time, Pallas kernels for 14%

profile of v3, /device:TPU:1, one launch (start us, length us, event | category | flops | bytes accessed | tf_op | source)
XLA Modules:
  0.0 170.7 jit_solution(6251669629911006227)
XLA Ops:
  0.6 0.0 copy-start
  0.6 1.9 %copy-done = bf16[32,64,768]{2,1,0:T(8,128)(2,1)S(1)} copy-done((bf16[32,64,768]{2,1,0:T(8,128)(2,1)S(1)}, bf16[32,64,768]{2,1,0:T(8,128)(2,1)}, u32[]{:S(2)}) %copy-start) | copy-done | bytes 3145752
  2.5 0.0 copy-start.2
  2.5 0.5 local_squares.1
  3.1 28.2 %all_to_all.25.squares_ref = f32[256,1,128]{2,1,0:T(1,128)S(1)} all-to-all(f32[256,1,128]{2,1,0:T(1,128)S(1)} %local_squares.1), channel_id=1, replica_groups=mesh['zh'=2,'x'=4,'y'=4,'far'=2,'near'=2,'core'=2] {'zh','x','y','far','..., dimensions={0} | all-to-all | bytes 262144 | tf_op jit(solution)/shard_map/all_to_all | solution.py:324
  31.3 0.0 copy-done.2
  31.3 1.6 first_step.1
  32.9 0.0 copy-start.1
  32.9 5.4 %all-to-all-start.1 = ((bf16[16,64,768]{2,1,0:T(8,128)(2,1)}), bf16[16,64,768]{2,1,0:T(8,128)(2,1)}, u32[]{:S(2)}, u32[]{:S(2)}) async-start(bf16[16,64,768]{2,1,0:T(8,128)(2,1)} %first_step.1), calls=%async_computation.1 | async-start | bytes 3145728 | tf_op jit(solution)/shard_map/all_to_all | solution.py:327
  38.4 0.0 copy-done.1
  38.4 0.0 copy-start.3
  38.4 1.9 %copy-done.3 = bf16[32,64,768]{2,1,0:T(8,128)(2,1)S(1)} copy-done((bf16[32,64,768]{2,1,0:T(8,128)(2,1)S(1)}, bf16[32,64,768]{2,1,0:T(8,128)(2,1)}, u32[]{:S(2)}) %copy-start.3) | copy-done | bytes 3145752
  40.3 6.0 %whole_step.1 = (bf16[32,64,768]{2,1,0:T(8,128)(2,1)}, bf16[16,64,768]{2,1,0:T(8,128)(2,1)}, f32[1,128]{1,0:T(1,128)S(1)}) custom-call(f32[256,1,128]{2,1,0:T(1,128)S(1)} %all_to_all.25.squares_ref, bf16[32,64,768]{2,1,0:T(8,128)(2,1)S(1)} %copy-done.3, bf16[32,64,768]{2,1,0:T(8,128)(2,1)S(1)} %copy-done.1), custom_call_target="tpu_custom_call" | custom-call | tf_op jit(solution)/shard_map/whole_step/pallas_call | solution.py:138
  46.2 0.3 collective-permute-start
  46.5 0.8 collective-permute-done
  47.4 1.5 collective-permute-start.1
  48.8 9.5 %collective-permute-done.1 = f32[1,128]{1,0:T(1,128)S(1)} collective-permute-done((f32[1,128]{1,0:T(1,128)S(1)}, f32[1,128]{1,0:T(1,128)S(1)}, u32[]{:S(2)}, u32[]{:S(2)}) %collective-permute-start.1) | collective-permute-done | bytes 544 | tf_op jit(solution)/shard_map/ppermute | solution.py:314
  58.3 1.7 %all-to-all-done.1 = bf16[16,64,768]{2,1,0:T(8,128)(2,1)} async-done(((bf16[16,64,768]{2,1,0:T(8,128)(2,1)}), bf16[16,64,768]{2,1,0:T(8,128)(2,1)}, u32[]{:S(2)}, u32[]{:S(2)}) %all-to-all-start.1) | async-done | bytes 1572896 | tf_op jit(solution)/shard_map/all_to_all | solution.py:327
  60.1 2.4 %partial_gram.2.own_ref = bf16[2320,128]{1,0:T(8,128)(2,1)S(1)} custom-call(bf16[1024,768]{1,0:T(8,128)(2,1)} %bitcast.m_ref, f32[1,128]{1,0:T(1,128)S(1)} %add.28.sums_ref), custom_call_target="tpu_custom_call" | custom-call | flops 1207959552 | bytes 2000000 | tf_op jit(solution)/shard_map/partial_gram/pallas_call | solution.py:224
  62.5 0.8 collective-permute-start.2
  63.3 4.7 %all-to-all-start.2 = ((bf16[16,64,768]{2,1,0:T(8,128)(2,1)}), bf16[16,64,768]{2,1,0:T(8,128)(2,1)S(1)}, u32[]{:S(2)}, u32[]{:S(2)}) async-start(bf16[16,64,768]{2,1,0:T(8,128)(2,1)} %get-tuple-element.21), calls=%async_computation.2 | async-start | bytes 3145728 | tf_op jit(solution)/shard_map/all_to_all | solution.py:327
  67.9 23.1 %collective-permute-done.2.other_ref = bf16[2320,128]{1,0:T(8,128)(2,1)S(1)} collective-permute-done((bf16[2320,128]{1,0:T(8,128)(2,1)S(1)}, bf16[2320,128]{1,0:T(8,128)(2,1)S(1)}, u32[]{:S(2)}, u32[]{:S(2)}) %collective-permute-start.2) | collective-permute-done | bytes 593952 | tf_op jit(solution)/shard_map/ppermute | solution.py:314
  91.0 8.8 %orthogonal_rows.2 = bf16[1024,768]{1,0:T(8,128)(2,1)} custom-call(bf16[1024,768]{1,0:T(8,128)(2,1)} %bitcast.m_ref, bf16[2320,128]{1,0:T(8,128)(2,1)S(1)} %partial_gram.2.own_ref, bf16[2320,128]{1,0:T(8,128)(2,1)S(1)} %collective-permute-done.2.other_ref), custom_call_target="tpu_custom_call" | custom-call | flops 60000002048 | bytes 6000000 | tf_op jit(solution)/shard_map/orthogonal_rows/pallas_call | solution.py:292
  99.9 2.2 %all-to-all-done.2 = bf16[16,64,768]{2,1,0:T(8,128)(2,1)S(1)} async-done(((bf16[16,64,768]{2,1,0:T(8,128)(2,1)}), bf16[16,64,768]{2,1,0:T(8,128)(2,1)S(1)}, u32[]{:S(2)}, u32[]{:S(2)}) %all-to-all-start.2) | async-done | bytes 1572896 | tf_op jit(solution)/shard_map/all_to_all | solution.py:327
  102.0 1.8 %partial_gram.3.own_ref = bf16[2320,128]{1,0:T(8,128)(2,1)} custom-call(bf16[1024,768]{1,0:T(8,128)(2,1)S(1)} %bitcast.6, f32[1,128]{1,0:T(1,128)S(1)} %bitcast.8), custom_call_target="tpu_custom_call" | custom-call | flops 1207959552 | bytes 2000000 | tf_op jit(solution)/shard_map/partial_gram/pallas_call | solution.py:224
  103.9 0.0 collective-permute-start.3
  103.9 4.5 %all-to-all-start.4 = ((bf16[16,64,768]{2,1,0:T(8,128)(2,1)}), bf16[16,64,768]{2,1,0:T(8,128)(2,1)S(1)}, u32[]{:S(2)}, u32[]{:S(2)}) async-start(bf16[16,64,768]{2,1,0:T(8,128)(2,1)} %bitcast.14), calls=%async_computation.4 | async-start | bytes 3145728 | tf_op jit(solution)/shard_map/all_to_all | solution.py:331
  108.4 22.2 %collective-permute-done.3.other_ref = bf16[2320,128]{1,0:T(8,128)(2,1)} collective-permute-done((bf16[2320,128]{1,0:T(8,128)(2,1)}, bf16[2320,128]{1,0:T(8,128)(2,1)}, u32[]{:S(2)}, u32[]{:S(2)}) %collective-permute-start.3) | collective-permute-done | bytes 593952 | tf_op jit(solution)/shard_map/ppermute | solution.py:314
  130.6 8.7 %orthogonal_rows.3 = bf16[1024,768]{1,0:T(8,128)(2,1)} custom-call(bf16[1024,768]{1,0:T(8,128)(2,1)S(1)} %bitcast.7, bf16[2320,128]{1,0:T(8,128)(2,1)} %partial_gram.3.own_ref, bf16[2320,128]{1,0:T(8,128)(2,1)} %collective-permute-done.3.other_ref), custom_call_target="tpu_custom_call" | custom-call | flops 60000002048 | bytes 6000000 | tf_op jit(solution)/shard_map/orthogonal_rows/pallas_call | solution.py:292
  139.3 3.1 %all-to-all-done.4.part_ref = bf16[16,64,768]{2,1,0:T(8,128)(2,1)S(1)} async-done(((bf16[16,64,768]{2,1,0:T(8,128)(2,1)}), bf16[16,64,768]{2,1,0:T(8,128)(2,1)S(1)}, u32[]{:S(2)}, u32[]{:S(2)}) %all-to-all-start.4) | async-done | bytes 1572896 | tf_op jit(solution)/shard_map/all_to_all | solution.py:331
  142.4 4.4 %all-to-all-start.3 = ((bf16[16,64,768]{2,1,0:T(8,128)(2,1)}), bf16[16,64,768]{2,1,0:T(8,128)(2,1)S(1)}, u32[]{:S(2)}, u32[]{:S(2)}) async-start(bf16[16,64,768]{2,1,0:T(8,128)(2,1)} %bitcast.13), calls=%async_computation.3 | async-start | bytes 3145728 | tf_op jit(solution)/shard_map/all_to_all | solution.py:331
  146.8 0.0 copy-start.4
  146.8 1.2 place.2.refs_0_
  148.0 1.5 collective-permute-start.4
  149.5 2.4 %collective-permute-start.5 = (f32[1,128]{1,0:T(1,128)S(1)}, f32[1,128]{1,0:T(1,128)S(1)}, u32[]{:S(2)}, u32[]{:S(2)}) collective-permute-start(f32[1,128]{1,0:T(1,128)S(1)} %bitcast.10), channel_id=1, source_target_pairs={{0,16},{8,24},{16,0},{24,8},{1,17},{9,25},{17,1},{25,9},{2,18},{10... | collective-permute-start | bytes 1544 | tf_op jit(solution)/shard_map/ppermute | solution.py:353
  151.9 1.2 collective-permute-start.6
  153.1 9.0 %collective-permute-done.4 = f32[1,128]{1,0:T(1,128)S(1)} collective-permute-done((f32[1,128]{1,0:T(1,128)S(1)}, f32[1,128]{1,0:T(1,128)S(1)}, u32[]{:S(2)}, u32[]{:S(2)}) %collective-permute-start.4) | collective-permute-done | bytes 544 | tf_op jit(solution)/shard_map/ppermute | solution.py:353
  162.1 3.4 %collective-permute-done.5 = f32[1,128]{1,0:T(1,128)S(1)} collective-permute-done((f32[1,128]{1,0:T(1,128)S(1)}, f32[1,128]{1,0:T(1,128)S(1)}, u32[]{:S(2)}, u32[]{:S(2)}) %collective-permute-start.5) | collective-permute-done | bytes 544 | tf_op jit(solution)/shard_map/ppermute | solution.py:353
  165.5 0.7 collective-permute-done.6
  166.1 0.0 copy-done.4
  166.1 0.6 fusion
  167.4 1.0 all-to-all-done.3.part_ref
  168.4 1.2 place.3
  (4 shorter events, 0.0 us)
Async XLA Ops:
  0.6 1.9 %copy-start = (bf16[32,64,768]{2,1,0:T(8,128)(2,1)S(1)}, bf16[32,64,768]{2,1,0:T(8,128)(2,1)}, u32[]{:S(2)}) copy-start(bf16[32,64,768]{2,1,0:T(8,128)(2,1)} %g_ref.5) | copy-start | bytes 9437188
  2.5 28.8 %copy-start.2 = (bf16[32,64,768]{2,1,0:T(8,128)(2,1)S(1)}, bf16[32,64,768]{2,1,0:T(8,128)(2,1)}, u32[]{:S(2)}) copy-start(bf16[32,64,768]{2,1,0:T(8,128)(2,1)} %m_ref.3) | copy-start | bytes 9437188
  32.9 5.5 %copy-start.1 = (bf16[32,64,768]{2,1,0:T(8,128)(2,1)S(1)}, bf16[32,64,768]{2,1,0:T(8,128)(2,1)}, u32[]{:S(2)}) copy-start(bf16[32,64,768]{2,1,0:T(8,128)(2,1)} %g_ref.5) | copy-start | bytes 9437188
  32.9 27.1 %all-to-all-start.1 = ((bf16[16,64,768]{2,1,0:T(8,128)(2,1)}), bf16[16,64,768]{2,1,0:T(8,128)(2,1)}, u32[]{:S(2)}, u32[]{:S(2)}) async-start(bf16[16,64,768]{2,1,0:T(8,128)(2,1)} %first_step.1), calls=%async_computation.1 | async-start | bytes 3145728 | tf_op jit(solution)/shard_map/all_to_all | solution.py:327
  38.4 1.9 %copy-start.3 = (bf16[32,64,768]{2,1,0:T(8,128)(2,1)S(1)}, bf16[32,64,768]{2,1,0:T(8,128)(2,1)}, u32[]{:S(2)}) copy-start(bf16[32,64,768]{2,1,0:T(8,128)(2,1)} %m_ref.3) | copy-start | bytes 9437188
  46.2 1.1 collective-permute-start
  47.4 11.0 %collective-permute-start.1 = (f32[1,128]{1,0:T(1,128)S(1)}, f32[1,128]{1,0:T(1,128)S(1)}, u32[]{:S(2)}, u32[]{:S(2)}) collective-permute-start(f32[1,128]{1,0:T(1,128)S(1)} %add.27), channel_id=1, source_target_pairs={{0,2},{2,0},{1,3},{3,1},{4,6},{6,4},{5,7},{7,5},{8,10},{10,8},{9,1... | collective-permute-start | bytes 1544 | tf_op jit(solution)/shard_map/ppermute | solution.py:314
  62.5 28.5 %collective-permute-start.2 = (bf16[2320,128]{1,0:T(8,128)(2,1)S(1)}, bf16[2320,128]{1,0:T(8,128)(2,1)S(1)}, u32[]{:S(2)}, u32[]{:S(2)}) collective-permute-start(bf16[2320,128]{1,0:T(8,128)(2,1)S(1)} %partial_gram.2.own_ref), channel_id=1, source_target_pairs={{0,4},{4,0},{1,5},{5,1},{2,6},{6,2},{3,7},{7,3},{8,12},{12,8},{9,1... | collective-permute-start | bytes 1781768 | tf_op jit(solution)/shard_map/ppermute | solution.py:314
  63.3 38.8 %all-to-all-start.2 = ((bf16[16,64,768]{2,1,0:T(8,128)(2,1)}), bf16[16,64,768]{2,1,0:T(8,128)(2,1)S(1)}, u32[]{:S(2)}, u32[]{:S(2)}) async-start(bf16[16,64,768]{2,1,0:T(8,128)(2,1)} %get-tuple-element.21), calls=%async_computation.2 | async-start | bytes 3145728 | tf_op jit(solution)/shard_map/all_to_all | solution.py:327
  103.9 26.7 %collective-permute-start.3 = (bf16[2320,128]{1,0:T(8,128)(2,1)}, bf16[2320,128]{1,0:T(8,128)(2,1)}, u32[]{:S(2)}, u32[]{:S(2)}) collective-permute-start(bf16[2320,128]{1,0:T(8,128)(2,1)} %partial_gram.3.own_ref), channel_id=1, source_target_pairs={{0,4},{4,0},{1,5},{5,1},{2,6},{6,2},{3,7},{7,3},{8,12},{12,8},{9,1... | collective-permute-start | bytes 1781768 | tf_op jit(solution)/shard_map/ppermute | solution.py:314
  103.9 38.5 %all-to-all-start.4 = ((bf16[16,64,768]{2,1,0:T(8,128)(2,1)}), bf16[16,64,768]{2,1,0:T(8,128)(2,1)S(1)}, u32[]{:S(2)}, u32[]{:S(2)}) async-start(bf16[16,64,768]{2,1,0:T(8,128)(2,1)} %bitcast.14), calls=%async_computation.4 | async-start | bytes 3145728 | tf_op jit(solution)/shard_map/all_to_all | solution.py:331
  142.4 26.0 %all-to-all-start.3 = ((bf16[16,64,768]{2,1,0:T(8,128)(2,1)}), bf16[16,64,768]{2,1,0:T(8,128)(2,1)S(1)}, u32[]{:S(2)}, u32[]{:S(2)}) async-start(bf16[16,64,768]{2,1,0:T(8,128)(2,1)} %bitcast.13), calls=%async_computation.3 | async-start | bytes 3145728 | tf_op jit(solution)/shard_map/all_to_all | solution.py:331
  146.8 19.3 %copy-start.4 = (s32[1,32]{1,0:T(1,128)S(1)}, s32[1,32]{1,0:T(1,128)}, u32[]{:S(2)}) copy-start(s32[1,32]{1,0:T(1,128)} %param.5) | copy-start | bytes 388
  148.0 14.1 %collective-permute-start.4 = (f32[1,128]{1,0:T(1,128)S(1)}, f32[1,128]{1,0:T(1,128)S(1)}, u32[]{:S(2)}, u32[]{:S(2)}) collective-permute-start(f32[1,128]{1,0:T(1,128)S(1)} %bitcast.9), channel_id=1, source_target_pairs={{0,8},{8,16},{16,24},{24,0},{1,9},{9,17},{17,25},{25,1},{2,10},{10... | collective-permute-start | bytes 1544 | tf_op jit(solution)/shard_map/ppermute | solution.py:353
  149.5 16.0 %collective-permute-start.5 = (f32[1,128]{1,0:T(1,128)S(1)}, f32[1,128]{1,0:T(1,128)S(1)}, u32[]{:S(2)}, u32[]{:S(2)}) collective-permute-start(f32[1,128]{1,0:T(1,128)S(1)} %bitcast.10), channel_id=1, source_target_pairs={{0,16},{8,24},{16,0},{24,8},{1,17},{9,25},{17,1},{25,9},{2,18},{10... | collective-permute-start | bytes 1544 | tf_op jit(solution)/shard_map/ppermute | solution.py:353
  151.9 14.2 %collective-permute-start.6 = (f32[1,128]{1,0:T(1,128)S(1)}, f32[1,128]{1,0:T(1,128)S(1)}, u32[]{:S(2)}, u32[]{:S(2)}) collective-permute-start(f32[1,128]{1,0:T(1,128)S(1)} %bitcast.11), channel_id=1, source_target_pairs={{0,24},{8,0},{16,8},{24,16},{1,25},{9,1},{17,9},{25,17},{2,26},{10... | collective-permute-start | bytes 1544 | tf_op jit(solution)/shard_map/ppermute | solution.py:353

commit v4 on v3

--- a/solution.py
+++ b/solution.py
@@ -145,7 +145,7 @@
             pltpu.HBM((count // 2,) + momentum.shape[1:], bf16),
             jax.ShapeDtypeStruct((1, B), f32),
         ],
-        compiler_params=pltpu.CompilerParams(vmem_limit_bytes=16 << 20),
+        compiler_params=pltpu.CompilerParams(vmem_limit_bytes=52 << 20),
         name="whole_step",
     )(squares, momentum, gradient)
 
@@ -227,7 +227,7 @@
         out_specs=VMEM,
         out_shape=jax.ShapeDtypeStruct((PACKED, B), bf16),
         scratch_shapes=[pltpu.VMEM((FF, FF), f32)],
-        compiler_params=pltpu.CompilerParams(vmem_limit_bytes=24 << 20),
+        compiler_params=pltpu.CompilerParams(vmem_limit_bytes=16 << 20),
         name="partial_gram",
         cost_estimate=pl.CostEstimate(flops=2 * part.shape[0] * FF * FF, bytes_accessed=2_000_000, transcendentals=0),
     )(part, sums)
@@ -304,7 +304,7 @@
             pltpu.VMEM(part.shape, bf16),
             pltpu.SemaphoreType.DMA((UPDATE_STRIPS,)),
         ],
-        compiler_params=pltpu.CompilerParams(vmem_limit_bytes=32 << 20),
+        compiler_params=pltpu.CompilerParams(vmem_limit_bytes=20 << 20),
         name="orthogonal_rows",
         cost_estimate=pl.CostEstimate(flops=60_000_000_000, bytes_accessed=6_000_000, transcendentals=0),
     )(part, own, other)

time: 171 us -> 170 us (level)
  local copies, waits for them, and re-layouts: 3.78 us -> 1.89 us
  Pallas kernels: 32.3 us -> 34.1 us
    pallas_call x1, Pallas kernels: 5.97 us -> 8.59 us  [whole_step(): pl.pallas_call(functools.partial(whole_step_kernel, entry_count), grid=(c...]
    unnamed x10 -> x6, local copies, waits for them, and re-layouts: 3.78 us -> 1.89 us
  transfers between devices with their start and end apart: 11 -> 11, of which waited for: 11 -> 11; matrix products, arithmetic and copies ran while one was open for 0% -> 1% of each run, Pallas kernels for 14% -> 16%
where the time goes in v4:
time: 170 us; the launch traced here: 169 us
  waiting for transfers between devices  75.4 us (44%)
  Pallas kernels  34.1 us (20%)
  blocking collectives  28.2 us (17%)
  starting transfers between devices  25.5 us (15%)
  between operations  2.53 us (1%)
  local copies, waits for them, and re-layouts  1.89 us (1%)
    ppermute x4, waiting for transfers between devices, swap(): return lax.ppermute(x, axis, [(0, 1), (1, 0)])  55.7 us
    all_to_all x1, blocking collectives, local(): lax.all_to_all(local_squares(gradient, everyone), AXES, 0, 0, tiled=True)  28.2 us
    pallas_call x2, Pallas kernels, orthogonal_rows(): pl.pallas_call(update_kernel, in_specs=[VMEM, VMEM, VMEM], out_specs=pl.B...  17.3 us
    ppermute x3, waiting for transfers between devices, local(): lax.ppermute(sums, 'y', [(i, (i + k) % 4) for i in range(4)])  13 us
    all_to_all x2, starting transfers between devices, gather(): rows = lax.all_to_all(part, HALF, 0, 0, tiled=True)  9.2 us
    all_to_all x2, starting transfers between devices, scatter(): lax.all_to_all(update.reshape(HALF_SIZE, row_count, FF), HALF, 0, 0, tile...  8.87 us
    pallas_call x1, Pallas kernels, whole_step(): pl.pallas_call(functools.partial(whole_step_kernel, entry_count), grid=(c...  8.59 us
    ppermute x3, starting transfers between devices, local(): lax.ppermute(sums, 'y', [(i, (i + k) % 4) for i in range(4)])  5.09 us
  transfers between devices with their start and end apart: 11, of which 11 were waited for; matrix products, arithmetic and copies ran while one was open for 1% of the time, Pallas kernels for 16%

profile of v4, /device:TPU:1, one launch (start us, length us, event | category | flops | bytes accessed | tf_op | source)
XLA Modules:
  0.0 169.0 jit_solution(10677023474239429563)
XLA Ops:
  0.6 0.0 copy-start
  0.6 1.9 %copy-done = bf16[32,64,768]{2,1,0:T(8,128)(2,1)S(1)} copy-done((bf16[32,64,768]{2,1,0:T(8,128)(2,1)S(1)}, bf16[32,64,768]{2,1,0:T(8,128)(2,1)}, u32[]{:S(2)}) %copy-start) | copy-done | bytes 3145752
  2.5 0.0 copy-start.1
  2.5 0.5 local_squares.1
  3.1 28.2 %all_to_all.25.squares_ref = f32[256,1,128]{2,1,0:T(1,128)S(1)} all-to-all(f32[256,1,128]{2,1,0:T(1,128)S(1)} %local_squares.1), channel_id=1, replica_groups=mesh['zh'=2,'x'=4,'y'=4,'far'=2,'near'=2,'core'=2] {'zh','x','y','far','..., dimensions={0} | all-to-all | bytes 262144 | tf_op jit(solution)/shard_map/all_to_all | solution.py:324
  31.3 0.0 copy-done.1
  31.3 1.6 first_step.1
  32.9 4.5 %all-to-all-start.1 = ((bf16[16,64,768]{2,1,0:T(8,128)(2,1)}), bf16[16,64,768]{2,1,0:T(8,128)(2,1)S(1)}, u32[]{:S(2)}, u32[]{:S(2)}) async-start(bf16[16,64,768]{2,1,0:T(8,128)(2,1)} %first_step.1), calls=%async_computation.1 | async-start | bytes 3145728 | tf_op jit(solution)/shard_map/all_to_all | solution.py:327
  37.4 8.6 %whole_step.1 = (bf16[32,64,768]{2,1,0:T(8,128)(2,1)}, bf16[16,64,768]{2,1,0:T(8,128)(2,1)}, f32[1,128]{1,0:T(1,128)S(1)}) custom-call(f32[256,1,128]{2,1,0:T(1,128)S(1)} %all_to_all.25.squares_ref, bf16[32,64,768]{2,1,0:T(8,128)(2,1)} %m_ref.3, bf16[32,64,768]{2,1,0:T(8,128)(2,1)} %g_ref.5), custom_call_target="tpu_custom_call" | custom-call | tf_op jit(solution)/shard_map/whole_step/pallas_call | solution.py:138
  46.0 0.2 collective-permute-start
  46.3 0.9 collective-permute-done
  47.2 1.5 collective-permute-start.1
  48.6 8.8 %collective-permute-done.1 = f32[1,128]{1,0:T(1,128)S(1)} collective-permute-done((f32[1,128]{1,0:T(1,128)S(1)}, f32[1,128]{1,0:T(1,128)S(1)}, u32[]{:S(2)}, u32[]{:S(2)}) %collective-permute-start.1) | collective-permute-done | bytes 544 | tf_op jit(solution)/shard_map/ppermute | solution.py:314
  57.4 1.6 all-to-all-done.1
  59.0 1.9 %partial_gram.2.own_ref = bf16[2320,128]{1,0:T(8,128)(2,1)} custom-call(bf16[1024,768]{1,0:T(8,128)(2,1)S(1)} %bitcast.6, f32[1,128]{1,0:T(1,128)S(1)} %add.28.sums_ref), custom_call_target="tpu_custom_call" | custom-call | flops 1207959552 | bytes 2000000 | tf_op jit(solution)/shard_map/partial_gram/pallas_call | solution.py:224
  60.9 0.7 collective-permute-start.2
  61.6 4.7 %all-to-all-start.2 = ((bf16[16,64,768]{2,1,0:T(8,128)(2,1)}), bf16[16,64,768]{2,1,0:T(8,128)(2,1)S(1)}, u32[]{:S(2)}, u32[]{:S(2)}) async-start(bf16[16,64,768]{2,1,0:T(8,128)(2,1)} %get-tuple-element.21), calls=%async_computation.2 | async-start | bytes 3145728 | tf_op jit(solution)/shard_map/all_to_all | solution.py:327
  66.3 23.4 %collective-permute-done.2.other_ref = bf16[2320,128]{1,0:T(8,128)(2,1)} collective-permute-done((bf16[2320,128]{1,0:T(8,128)(2,1)}, bf16[2320,128]{1,0:T(8,128)(2,1)}, u32[]{:S(2)}, u32[]{:S(2)}) %collective-permute-start.2) | collective-permute-done | bytes 593952 | tf_op jit(solution)/shard_map/ppermute | solution.py:314
  89.6 0.7 add_reduce_fusion
  90.3 8.7 %orthogonal_rows.2 = bf16[1024,768]{1,0:T(8,128)(2,1)} custom-call(bf16[1024,768]{1,0:T(8,128)(2,1)S(1)} %bitcast.7, bf16[2320,128]{1,0:T(8,128)(2,1)} %partial_gram.2.own_ref, bf16[2320,128]{1,0:T(8,128)(2,1)} %collective-permute-done.2.other_ref), custom_call_target="tpu_custom_call" | custom-call | flops 60000002048 | bytes 6000000 | tf_op jit(solution)/shard_map/orthogonal_rows/pallas_call | solution.py:292
  99.0 1.4 all-to-all-done.2
  100.4 1.8 %partial_gram.3.own_ref = bf16[2320,128]{1,0:T(8,128)(2,1)} custom-call(bf16[1024,768]{1,0:T(8,128)(2,1)S(1)} %bitcast.8, f32[1,128]{1,0:T(1,128)S(1)} %bitcast.10), custom_call_target="tpu_custom_call" | custom-call | flops 1207959552 | bytes 2000000 | tf_op jit(solution)/shard_map/partial_gram/pallas_call | solution.py:224
  102.2 0.0 collective-permute-start.3
  102.2 4.5 %all-to-all-start.4 = ((bf16[16,64,768]{2,1,0:T(8,128)(2,1)}), bf16[16,64,768]{2,1,0:T(8,128)(2,1)S(1)}, u32[]{:S(2)}, u32[]{:S(2)}) async-start(bf16[16,64,768]{2,1,0:T(8,128)(2,1)} %bitcast.16), calls=%async_computation.4 | async-start | bytes 3145728 | tf_op jit(solution)/shard_map/all_to_all | solution.py:331
  106.7 22.6 %collective-permute-done.3.other_ref = bf16[2320,128]{1,0:T(8,128)(2,1)} collective-permute-done((bf16[2320,128]{1,0:T(8,128)(2,1)}, bf16[2320,128]{1,0:T(8,128)(2,1)}, u32[]{:S(2)}, u32[]{:S(2)}) %collective-permute-start.3) | collective-permute-done | bytes 593952 | tf_op jit(solution)/shard_map/ppermute | solution.py:314
  129.3 8.7 %orthogonal_rows.3 = bf16[1024,768]{1,0:T(8,128)(2,1)} custom-call(bf16[1024,768]{1,0:T(8,128)(2,1)S(1)} %bitcast.9, bf16[2320,128]{1,0:T(8,128)(2,1)} %partial_gram.3.own_ref, bf16[2320,128]{1,0:T(8,128)(2,1)} %collective-permute-done.3.other_ref), custom_call_target="tpu_custom_call" | custom-call | flops 60000002048 | bytes 6000000 | tf_op jit(solution)/shard_map/orthogonal_rows/pallas_call | solution.py:292
  138.0 2.8 %all-to-all-done.4.part_ref = bf16[16,64,768]{2,1,0:T(8,128)(2,1)S(1)} async-done(((bf16[16,64,768]{2,1,0:T(8,128)(2,1)}), bf16[16,64,768]{2,1,0:T(8,128)(2,1)S(1)}, u32[]{:S(2)}, u32[]{:S(2)}) %all-to-all-start.4) | async-done | bytes 1572896 | tf_op jit(solution)/shard_map/all_to_all | solution.py:331
  140.8 4.4 %all-to-all-start.3 = ((bf16[16,64,768]{2,1,0:T(8,128)(2,1)}), bf16[16,64,768]{2,1,0:T(8,128)(2,1)S(1)}, u32[]{:S(2)}, u32[]{:S(2)}) async-start(bf16[16,64,768]{2,1,0:T(8,128)(2,1)} %bitcast.15), calls=%async_computation.3 | async-start | bytes 3145728 | tf_op jit(solution)/shard_map/all_to_all | solution.py:331
  145.1 0.0 copy-start.2
  145.1 1.2 place.2.refs_0_
  146.3 1.5 collective-permute-start.4
  147.8 2.4 %collective-permute-start.5 = (f32[1,128]{1,0:T(1,128)S(1)}, f32[1,128]{1,0:T(1,128)S(1)}, u32[]{:S(2)}, u32[]{:S(2)}) collective-permute-start(f32[1,128]{1,0:T(1,128)S(1)} %bitcast.12), channel_id=1, source_target_pairs={{0,16},{8,24},{16,0},{24,8},{1,17},{9,25},{17,1},{25,9},{2,18},{10... | collective-permute-start | bytes 1544 | tf_op jit(solution)/shard_map/ppermute | solution.py:353
  150.2 1.2 collective-permute-start.6
  151.4 9.0 %collective-permute-done.4 = f32[1,128]{1,0:T(1,128)S(1)} collective-permute-done((f32[1,128]{1,0:T(1,128)S(1)}, f32[1,128]{1,0:T(1,128)S(1)}, u32[]{:S(2)}, u32[]{:S(2)}) %collective-permute-start.4) | collective-permute-done | bytes 544 | tf_op jit(solution)/shard_map/ppermute | solution.py:353
  160.4 3.4 %collective-permute-done.5 = f32[1,128]{1,0:T(1,128)S(1)} collective-permute-done((f32[1,128]{1,0:T(1,128)S(1)}, f32[1,128]{1,0:T(1,128)S(1)}, u32[]{:S(2)}, u32[]{:S(2)}) %collective-permute-start.5) | collective-permute-done | bytes 544 | tf_op jit(solution)/shard_map/ppermute | solution.py:353
  163.8 0.7 collective-permute-done.6
  164.4 0.0 copy-done.2
  164.5 0.6 fusion
  165.7 1.0 all-to-all-done.3.part_ref
  166.7 1.2 place.3
  (3 shorter events, 0.0 us)
Async XLA Ops:
  0.6 1.9 %copy-start = (bf16[32,64,768]{2,1,0:T(8,128)(2,1)S(1)}, bf16[32,64,768]{2,1,0:T(8,128)(2,1)}, u32[]{:S(2)}) copy-start(bf16[32,64,768]{2,1,0:T(8,128)(2,1)} %g_ref.5) | copy-start | bytes 9437188
  2.5 28.8 %copy-start.1 = (bf16[32,64,768]{2,1,0:T(8,128)(2,1)S(1)}, bf16[32,64,768]{2,1,0:T(8,128)(2,1)}, u32[]{:S(2)}) copy-start(bf16[32,64,768]{2,1,0:T(8,128)(2,1)} %m_ref.3) | copy-start | bytes 9437188
  32.9 26.1 %all-to-all-start.1 = ((bf16[16,64,768]{2,1,0:T(8,128)(2,1)}), bf16[16,64,768]{2,1,0:T(8,128)(2,1)S(1)}, u32[]{:S(2)}, u32[]{:S(2)}) async-start(bf16[16,64,768]{2,1,0:T(8,128)(2,1)} %first_step.1), calls=%async_computation.1 | async-start | bytes 3145728 | tf_op jit(solution)/shard_map/all_to_all | solution.py:327
  46.0 1.1 collective-permute-start
  47.2 10.3 %collective-permute-start.1 = (f32[1,128]{1,0:T(1,128)S(1)}, f32[1,128]{1,0:T(1,128)S(1)}, u32[]{:S(2)}, u32[]{:S(2)}) collective-permute-start(f32[1,128]{1,0:T(1,128)S(1)} %add.27), channel_id=1, source_target_pairs={{0,2},{2,0},{1,3},{3,1},{4,6},{6,4},{5,7},{7,5},{8,10},{10,8},{9,1... | collective-permute-start | bytes 1544 | tf_op jit(solution)/shard_map/ppermute | solution.py:314
  60.9 28.7 %collective-permute-start.2 = (bf16[2320,128]{1,0:T(8,128)(2,1)}, bf16[2320,128]{1,0:T(8,128)(2,1)}, u32[]{:S(2)}, u32[]{:S(2)}) collective-permute-start(bf16[2320,128]{1,0:T(8,128)(2,1)} %partial_gram.2.own_ref), channel_id=1, source_target_pairs={{0,4},{4,0},{1,5},{5,1},{2,6},{6,2},{3,7},{7,3},{8,12},{12,8},{9,1... | collective-permute-start | bytes 1781768 | tf_op jit(solution)/shard_map/ppermute | solution.py:314
  61.6 38.8 %all-to-all-start.2 = ((bf16[16,64,768]{2,1,0:T(8,128)(2,1)}), bf16[16,64,768]{2,1,0:T(8,128)(2,1)S(1)}, u32[]{:S(2)}, u32[]{:S(2)}) async-start(bf16[16,64,768]{2,1,0:T(8,128)(2,1)} %get-tuple-element.21), calls=%async_computation.2 | async-start | bytes 3145728 | tf_op jit(solution)/shard_map/all_to_all | solution.py:327
  102.2 27.1 %collective-permute-start.3 = (bf16[2320,128]{1,0:T(8,128)(2,1)}, bf16[2320,128]{1,0:T(8,128)(2,1)}, u32[]{:S(2)}, u32[]{:S(2)}) collective-permute-start(bf16[2320,128]{1,0:T(8,128)(2,1)} %partial_gram.3.own_ref), channel_id=1, source_target_pairs={{0,4},{4,0},{1,5},{5,1},{2,6},{6,2},{3,7},{7,3},{8,12},{12,8},{9,1... | collective-permute-start | bytes 1781768 | tf_op jit(solution)/shard_map/ppermute | solution.py:314
  102.2 38.5 %all-to-all-start.4 = ((bf16[16,64,768]{2,1,0:T(8,128)(2,1)}), bf16[16,64,768]{2,1,0:T(8,128)(2,1)S(1)}, u32[]{:S(2)}, u32[]{:S(2)}) async-start(bf16[16,64,768]{2,1,0:T(8,128)(2,1)} %bitcast.16), calls=%async_computation.4 | async-start | bytes 3145728 | tf_op jit(solution)/shard_map/all_to_all | solution.py:331
  140.8 26.0 %all-to-all-start.3 = ((bf16[16,64,768]{2,1,0:T(8,128)(2,1)}), bf16[16,64,768]{2,1,0:T(8,128)(2,1)S(1)}, u32[]{:S(2)}, u32[]{:S(2)}) async-start(bf16[16,64,768]{2,1,0:T(8,128)(2,1)} %bitcast.15), calls=%async_computation.3 | async-start | bytes 3145728 | tf_op jit(solution)/shard_map/all_to_all | solution.py:331
  145.1 19.3 %copy-start.2 = (s32[1,32]{1,0:T(1,128)S(1)}, s32[1,32]{1,0:T(1,128)}, u32[]{:S(2)}) copy-start(s32[1,32]{1,0:T(1,128)} %param.5) | copy-start | bytes 388
  146.3 14.1 %collective-permute-start.4 = (f32[1,128]{1,0:T(1,128)S(1)}, f32[1,128]{1,0:T(1,128)S(1)}, u32[]{:S(2)}, u32[]{:S(2)}) collective-permute-start(f32[1,128]{1,0:T(1,128)S(1)} %bitcast.11), channel_id=1, source_target_pairs={{0,8},{8,16},{16,24},{24,0},{1,9},{9,17},{17,25},{25,1},{2,10},{10... | collective-permute-start | bytes 1544 | tf_op jit(solution)/shard_map/ppermute | solution.py:353
  147.8 16.0 %collective-permute-start.5 = (f32[1,128]{1,0:T(1,128)S(1)}, f32[1,128]{1,0:T(1,128)S(1)}, u32[]{:S(2)}, u32[]{:S(2)}) collective-permute-start(f32[1,128]{1,0:T(1,128)S(1)} %bitcast.12), channel_id=1, source_target_pairs={{0,16},{8,24},{16,0},{24,8},{1,17},{9,25},{17,1},{25,9},{2,18},{10... | collective-permute-start | bytes 1544 | tf_op jit(solution)/shard_map/ppermute | solution.py:353
  150.2 14.2 %collective-permute-start.6 = (f32[1,128]{1,0:T(1,128)S(1)}, f32[1,128]{1,0:T(1,128)S(1)}, u32[]{:S(2)}, u32[]{:S(2)}) collective-permute-start(f32[1,128]{1,0:T(1,128)S(1)} %bitcast.13), channel_id=1, source_target_pairs={{0,24},{8,0},{16,8},{24,16},{1,25},{9,1},{17,9},{25,17},{2,26},{10... | collective-permute-start | bytes 1544 | tf_op jit(solution)/shard_map/ppermute | solution.py:353

commit v5 on v3

--- a/solution.py
+++ b/solution.py
@@ -36,37 +36,25 @@
 VMEM = pl.BlockSpec(memory_space=pltpu.VMEM)
 
 
-def square_kernel(g_ref, out_ref, acc):
-    step = pl.program_id(0)
-
-    @pl.when(step == 0)
-    def _():
-        acc[...] = jnp.zeros_like(acc)
-
+def square_kernel(g_ref, out_ref):
     def body(k, total):
         values = g_ref[k].astype(f32)
         return total + jnp.sum((values * values).reshape(-1, 8, FF), axis=0)
 
-    acc[...] = lax.fori_loop(0, g_ref.shape[0], body, acc[...])
-
-    @pl.when(step == pl.num_programs(0) - 1)
-    def _():
-        total = acc[:, 0:B]
-        for j in range(1, NB):
-            total = total + acc[:, j * B : (j + 1) * B]
-        total = jnp.sum(total, axis=0, keepdims=True)
-        out_ref[...] = jnp.broadcast_to(total[None], out_ref.shape)
+    acc = lax.fori_loop(0, g_ref.shape[0], body, jnp.zeros((8, FF), f32))
+    total = acc[:, 0:B]
+    for j in range(1, NB):
+        total = total + acc[:, j * B : (j + 1) * B]
+    total = jnp.sum(total, axis=0, keepdims=True)
+    out_ref[...] = jnp.broadcast_to(total[None], out_ref.shape)
 
 
 def local_squares(gradient, copies):
-    count = gradient.shape[0]
     return pl.pallas_call(
         square_kernel,
-        grid=(4,),
-        in_specs=[pl.BlockSpec((count // 4,) + gradient.shape[1:], lambda i: (i, 0, 0))],
-        out_specs=pl.BlockSpec((copies, 1, B), lambda i: (0, 0, 0)),
+        in_specs=[VMEM],
+        out_specs=VMEM,
         out_shape=jax.ShapeDtypeStruct((copies, 1, B), f32),
-        scratch_shapes=[pltpu.VMEM((8, FF), f32)],
         compiler_params=pltpu.CompilerParams(vmem_limit_bytes=16 << 20),
         name="local_squares",
     )(gradient)
@@ -145,7 +133,7 @@
             pltpu.HBM((count // 2,) + momentum.shape[1:], bf16),
             jax.ShapeDtypeStruct((1, B), f32),
         ],
-        compiler_params=pltpu.CompilerParams(vmem_limit_bytes=16 << 20),
+        compiler_params=pltpu.CompilerParams(vmem_limit_bytes=52 << 20),
         name="whole_step",
     )(squares, momentum, gradient)
 

time: 171 us -> 170 us (level)
  local copies, waits for them, and re-layouts: 3.78 us -> 1.89 us
    pallas_call x1, Pallas kernels: 5.97 us -> 8.59 us  [whole_step(): pl.pallas_call(functools.partial(whole_step_kernel, entry_count), grid=(c...]
    unnamed x10 -> x6, local copies, waits for them, and re-layouts: 3.78 us -> 1.89 us
  transfers between devices with their start and end apart: 11 -> 11, of which waited for: 11 -> 11; matrix products, arithmetic and copies ran while one was open for 0% -> 1% of each run, Pallas kernels for 14% -> 16%
where the time goes in v5:
time: 170 us; the launch traced here: 169 us
  waiting for transfers between devices  75.4 us (44%)
  Pallas kernels  34 us (20%)
  blocking collectives  28.2 us (17%)
  starting transfers between devices  25.5 us (15%)
  between operations  2.52 us (1%)
  local copies, waits for them, and re-layouts  1.89 us (1%)
    ppermute x4, waiting for transfers between devices, swap(): return lax.ppermute(x, axis, [(0, 1), (1, 0)])  55.7 us
    all_to_all x1, blocking collectives, local(): lax.all_to_all(local_squares(gradient, everyone), AXES, 0, 0, tiled=True)  28.2 us
    pallas_call x2, Pallas kernels, orthogonal_rows(): pl.pallas_call(update_kernel, in_specs=[VMEM, VMEM, VMEM], out_specs=pl.B...  17.3 us
    ppermute x3, waiting for transfers between devices, local(): lax.ppermute(sums, 'y', [(i, (i + k) % 4) for i in range(4)])  13 us
    all_to_all x2, starting transfers between devices, gather(): rows = lax.all_to_all(part, HALF, 0, 0, tiled=True)  9.19 us
    all_to_all x2, starting transfers between devices, scatter(): lax.all_to_all(update.reshape(HALF_SIZE, row_count, FF), HALF, 0, 0, tile...  8.87 us
    pallas_call x1, Pallas kernels, whole_step(): pl.pallas_call(functools.partial(whole_step_kernel, entry_count), grid=(c...  8.59 us
    ppermute x3, starting transfers between devices, local(): lax.ppermute(sums, 'y', [(i, (i + k) % 4) for i in range(4)])  5.09 us
  transfers between devices with their start and end apart: 11, of which 11 were waited for; matrix products, arithmetic and copies ran while one was open for 1% of the time, Pallas kernels for 16%

profile of v5, /device:TPU:1, one launch (start us, length us, event | category | flops | bytes accessed | tf_op | source)
XLA Modules:
  0.0 168.9 jit_solution(5021615667445433217)
XLA Ops:
  0.6 0.0 copy-start
  0.6 1.9 %copy-done = bf16[32,64,768]{2,1,0:T(8,128)(2,1)S(1)} copy-done((bf16[32,64,768]{2,1,0:T(8,128)(2,1)S(1)}, bf16[32,64,768]{2,1,0:T(8,128)(2,1)}, u32[]{:S(2)}) %copy-start) | copy-done | bytes 3145752
  2.5 0.0 copy-start.1
  2.5 0.5 local_squares.1
  3.0 28.2 %all_to_all.25.squares_ref = f32[256,1,128]{2,1,0:T(1,128)S(1)} all-to-all(f32[256,1,128]{2,1,0:T(1,128)S(1)} %local_squares.1), channel_id=1, replica_groups=mesh['zh'=2,'x'=4,'y'=4,'far'=2,'near'=2,'core'=2] {'zh','x','y','far','..., dimensions={0} | all-to-all | bytes 262144 | tf_op jit(solution)/shard_map/all_to_all | solution.py:312
  31.2 0.0 copy-done.1
  31.2 1.6 first_step.1
  32.8 4.5 %all-to-all-start.1 = ((bf16[16,64,768]{2,1,0:T(8,128)(2,1)}), bf16[16,64,768]{2,1,0:T(8,128)(2,1)S(1)}, u32[]{:S(2)}, u32[]{:S(2)}) async-start(bf16[16,64,768]{2,1,0:T(8,128)(2,1)} %first_step.1), calls=%async_computation.1 | async-start | bytes 3145728 | tf_op jit(solution)/shard_map/all_to_all | solution.py:315
  37.4 8.6 %whole_step.1 = (bf16[32,64,768]{2,1,0:T(8,128)(2,1)}, bf16[16,64,768]{2,1,0:T(8,128)(2,1)}, f32[1,128]{1,0:T(1,128)S(1)}) custom-call(f32[256,1,128]{2,1,0:T(1,128)S(1)} %all_to_all.25.squares_ref, bf16[32,64,768]{2,1,0:T(8,128)(2,1)} %m_ref.3, bf16[32,64,768]{2,1,0:T(8,128)(2,1)} %g_ref.5), custom_call_target="tpu_custom_call" | custom-call | tf_op jit(solution)/shard_map/whole_step/pallas_call | solution.py:126
  46.0 0.2 collective-permute-start
  46.2 0.9 collective-permute-done
  47.1 1.5 collective-permute-start.1
  48.5 8.8 %collective-permute-done.1 = f32[1,128]{1,0:T(1,128)S(1)} collective-permute-done((f32[1,128]{1,0:T(1,128)S(1)}, f32[1,128]{1,0:T(1,128)S(1)}, u32[]{:S(2)}, u32[]{:S(2)}) %collective-permute-start.1) | collective-permute-done | bytes 544 | tf_op jit(solution)/shard_map/ppermute | solution.py:302
  57.3 1.6 all-to-all-done.1
  59.0 1.9 %partial_gram.2.own_ref = bf16[2320,128]{1,0:T(8,128)(2,1)} custom-call(bf16[1024,768]{1,0:T(8,128)(2,1)S(1)} %bitcast.6, f32[1,128]{1,0:T(1,128)S(1)} %add.28.sums_ref), custom_call_target="tpu_custom_call" | custom-call | flops 1207959552 | bytes 2000000 | tf_op jit(solution)/shard_map/partial_gram/pallas_call | solution.py:212
  60.8 0.7 collective-permute-start.2
  61.5 4.6 %all-to-all-start.2 = ((bf16[16,64,768]{2,1,0:T(8,128)(2,1)}), bf16[16,64,768]{2,1,0:T(8,128)(2,1)S(1)}, u32[]{:S(2)}, u32[]{:S(2)}) async-start(bf16[16,64,768]{2,1,0:T(8,128)(2,1)} %get-tuple-element.21), calls=%async_computation.2 | async-start | bytes 3145728 | tf_op jit(solution)/shard_map/all_to_all | solution.py:315
  66.2 23.4 %collective-permute-done.2.other_ref = bf16[2320,128]{1,0:T(8,128)(2,1)} collective-permute-done((bf16[2320,128]{1,0:T(8,128)(2,1)}, bf16[2320,128]{1,0:T(8,128)(2,1)}, u32[]{:S(2)}, u32[]{:S(2)}) %collective-permute-start.2) | collective-permute-done | bytes 593952 | tf_op jit(solution)/shard_map/ppermute | solution.py:302
  89.6 0.7 add_reduce_fusion
  90.3 8.7 %orthogonal_rows.2 = bf16[1024,768]{1,0:T(8,128)(2,1)} custom-call(bf16[1024,768]{1,0:T(8,128)(2,1)S(1)} %bitcast.7, bf16[2320,128]{1,0:T(8,128)(2,1)} %partial_gram.2.own_ref, bf16[2320,128]{1,0:T(8,128)(2,1)} %collective-permute-done.2.other_ref), custom_call_target="tpu_custom_call" | custom-call | flops 60000002048 | bytes 6000000 | tf_op jit(solution)/shard_map/orthogonal_rows/pallas_call | solution.py:280
  98.9 1.4 all-to-all-done.2
  100.3 1.8 %partial_gram.3.own_ref = bf16[2320,128]{1,0:T(8,128)(2,1)} custom-call(bf16[1024,768]{1,0:T(8,128)(2,1)S(1)} %bitcast.8, f32[1,128]{1,0:T(1,128)S(1)} %bitcast.10), custom_call_target="tpu_custom_call" | custom-call | flops 1207959552 | bytes 2000000 | tf_op jit(solution)/shard_map/partial_gram/pallas_call | solution.py:212
  102.1 0.0 collective-permute-start.3
  102.1 4.5 %all-to-all-start.4 = ((bf16[16,64,768]{2,1,0:T(8,128)(2,1)}), bf16[16,64,768]{2,1,0:T(8,128)(2,1)S(1)}, u32[]{:S(2)}, u32[]{:S(2)}) async-start(bf16[16,64,768]{2,1,0:T(8,128)(2,1)} %bitcast.16), calls=%async_computation.4 | async-start | bytes 3145728 | tf_op jit(solution)/shard_map/all_to_all | solution.py:319
  106.6 22.6 %collective-permute-done.3.other_ref = bf16[2320,128]{1,0:T(8,128)(2,1)} collective-permute-done((bf16[2320,128]{1,0:T(8,128)(2,1)}, bf16[2320,128]{1,0:T(8,128)(2,1)}, u32[]{:S(2)}, u32[]{:S(2)}) %collective-permute-start.3) | collective-permute-done | bytes 593952 | tf_op jit(solution)/shard_map/ppermute | solution.py:302
  129.2 8.7 %orthogonal_rows.3 = bf16[1024,768]{1,0:T(8,128)(2,1)} custom-call(bf16[1024,768]{1,0:T(8,128)(2,1)S(1)} %bitcast.9, bf16[2320,128]{1,0:T(8,128)(2,1)} %partial_gram.3.own_ref, bf16[2320,128]{1,0:T(8,128)(2,1)} %collective-permute-done.3.other_ref), custom_call_target="tpu_custom_call" | custom-call | flops 60000002048 | bytes 6000000 | tf_op jit(solution)/shard_map/orthogonal_rows/pallas_call | solution.py:280
  137.9 2.8 %all-to-all-done.4.part_ref = bf16[16,64,768]{2,1,0:T(8,128)(2,1)S(1)} async-done(((bf16[16,64,768]{2,1,0:T(8,128)(2,1)}), bf16[16,64,768]{2,1,0:T(8,128)(2,1)S(1)}, u32[]{:S(2)}, u32[]{:S(2)}) %all-to-all-start.4) | async-done | bytes 1572896 | tf_op jit(solution)/shard_map/all_to_all | solution.py:319
  140.7 4.4 %all-to-all-start.3 = ((bf16[16,64,768]{2,1,0:T(8,128)(2,1)}), bf16[16,64,768]{2,1,0:T(8,128)(2,1)S(1)}, u32[]{:S(2)}, u32[]{:S(2)}) async-start(bf16[16,64,768]{2,1,0:T(8,128)(2,1)} %bitcast.15), calls=%async_computation.3 | async-start | bytes 3145728 | tf_op jit(solution)/shard_map/all_to_all | solution.py:319
  145.1 0.0 copy-start.2
  145.1 1.2 place.2.refs_0_
  146.2 1.5 collective-permute-start.4
  147.7 2.4 %collective-permute-start.5 = (f32[1,128]{1,0:T(1,128)S(1)}, f32[1,128]{1,0:T(1,128)S(1)}, u32[]{:S(2)}, u32[]{:S(2)}) collective-permute-start(f32[1,128]{1,0:T(1,128)S(1)} %bitcast.12), channel_id=1, source_target_pairs={{0,16},{8,24},{16,0},{24,8},{1,17},{9,25},{17,1},{25,9},{2,18},{10... | collective-permute-start | bytes 1544 | tf_op jit(solution)/shard_map/ppermute | solution.py:341
  150.2 1.2 collective-permute-start.6
  151.3 9.0 %collective-permute-done.4 = f32[1,128]{1,0:T(1,128)S(1)} collective-permute-done((f32[1,128]{1,0:T(1,128)S(1)}, f32[1,128]{1,0:T(1,128)S(1)}, u32[]{:S(2)}, u32[]{:S(2)}) %collective-permute-start.4) | collective-permute-done | bytes 544 | tf_op jit(solution)/shard_map/ppermute | solution.py:341
  160.3 3.4 %collective-permute-done.5 = f32[1,128]{1,0:T(1,128)S(1)} collective-permute-done((f32[1,128]{1,0:T(1,128)S(1)}, f32[1,128]{1,0:T(1,128)S(1)}, u32[]{:S(2)}, u32[]{:S(2)}) %collective-permute-start.5) | collective-permute-done | bytes 544 | tf_op jit(solution)/shard_map/ppermute | solution.py:341
  163.7 0.7 collective-permute-done.6
  164.4 0.0 copy-done.2
  164.4 0.6 fusion
  165.7 1.0 all-to-all-done.3.part_ref
  166.6 1.2 place.3
  (3 shorter events, 0.0 us)
Async XLA Ops:
  0.6 1.9 %copy-start = (bf16[32,64,768]{2,1,0:T(8,128)(2,1)S(1)}, bf16[32,64,768]{2,1,0:T(8,128)(2,1)}, u32[]{:S(2)}) copy-start(bf16[32,64,768]{2,1,0:T(8,128)(2,1)} %g_ref.5) | copy-start | bytes 9437188
  2.5 28.7 %copy-start.1 = (bf16[32,64,768]{2,1,0:T(8,128)(2,1)S(1)}, bf16[32,64,768]{2,1,0:T(8,128)(2,1)}, u32[]{:S(2)}) copy-start(bf16[32,64,768]{2,1,0:T(8,128)(2,1)} %m_ref.3) | copy-start | bytes 9437188
  32.8 26.1 %all-to-all-start.1 = ((bf16[16,64,768]{2,1,0:T(8,128)(2,1)}), bf16[16,64,768]{2,1,0:T(8,128)(2,1)S(1)}, u32[]{:S(2)}, u32[]{:S(2)}) async-start(bf16[16,64,768]{2,1,0:T(8,128)(2,1)} %first_step.1), calls=%async_computation.1 | async-start | bytes 3145728 | tf_op jit(solution)/shard_map/all_to_all | solution.py:315
  46.0 1.1 collective-permute-start
  47.1 10.3 %collective-permute-start.1 = (f32[1,128]{1,0:T(1,128)S(1)}, f32[1,128]{1,0:T(1,128)S(1)}, u32[]{:S(2)}, u32[]{:S(2)}) collective-permute-start(f32[1,128]{1,0:T(1,128)S(1)} %add.27), channel_id=1, source_target_pairs={{0,2},{2,0},{1,3},{3,1},{4,6},{6,4},{5,7},{7,5},{8,10},{10,8},{9,1... | collective-permute-start | bytes 1544 | tf_op jit(solution)/shard_map/ppermute | solution.py:302
  60.8 28.7 %collective-permute-start.2 = (bf16[2320,128]{1,0:T(8,128)(2,1)}, bf16[2320,128]{1,0:T(8,128)(2,1)}, u32[]{:S(2)}, u32[]{:S(2)}) collective-permute-start(bf16[2320,128]{1,0:T(8,128)(2,1)} %partial_gram.2.own_ref), channel_id=1, source_target_pairs={{0,4},{4,0},{1,5},{5,1},{2,6},{6,2},{3,7},{7,3},{8,12},{12,8},{9,1... | collective-permute-start | bytes 1781768 | tf_op jit(solution)/shard_map/ppermute | solution.py:302
  61.5 38.8 %all-to-all-start.2 = ((bf16[16,64,768]{2,1,0:T(8,128)(2,1)}), bf16[16,64,768]{2,1,0:T(8,128)(2,1)S(1)}, u32[]{:S(2)}, u32[]{:S(2)}) async-start(bf16[16,64,768]{2,1,0:T(8,128)(2,1)} %get-tuple-element.21), calls=%async_computation.2 | async-start | bytes 3145728 | tf_op jit(solution)/shard_map/all_to_all | solution.py:315
  102.1 27.1 %collective-permute-start.3 = (bf16[2320,128]{1,0:T(8,128)(2,1)}, bf16[2320,128]{1,0:T(8,128)(2,1)}, u32[]{:S(2)}, u32[]{:S(2)}) collective-permute-start(bf16[2320,128]{1,0:T(8,128)(2,1)} %partial_gram.3.own_ref), channel_id=1, source_target_pairs={{0,4},{4,0},{1,5},{5,1},{2,6},{6,2},{3,7},{7,3},{8,12},{12,8},{9,1... | collective-permute-start | bytes 1781768 | tf_op jit(solution)/shard_map/ppermute | solution.py:302
  102.1 38.5 %all-to-all-start.4 = ((bf16[16,64,768]{2,1,0:T(8,128)(2,1)}), bf16[16,64,768]{2,1,0:T(8,128)(2,1)S(1)}, u32[]{:S(2)}, u32[]{:S(2)}) async-start(bf16[16,64,768]{2,1,0:T(8,128)(2,1)} %bitcast.16), calls=%async_computation.4 | async-start | bytes 3145728 | tf_op jit(solution)/shard_map/all_to_all | solution.py:319
  140.7 26.0 %all-to-all-start.3 = ((bf16[16,64,768]{2,1,0:T(8,128)(2,1)}), bf16[16,64,768]{2,1,0:T(8,128)(2,1)S(1)}, u32[]{:S(2)}, u32[]{:S(2)}) async-start(bf16[16,64,768]{2,1,0:T(8,128)(2,1)} %bitcast.15), calls=%async_computation.3 | async-start | bytes 3145728 | tf_op jit(solution)/shard_map/all_to_all | solution.py:319
  145.1 19.3 %copy-start.2 = (s32[1,32]{1,0:T(1,128)S(1)}, s32[1,32]{1,0:T(1,128)}, u32[]{:S(2)}) copy-start(s32[1,32]{1,0:T(1,128)} %param.5) | copy-start | bytes 388
  146.2 14.1 %collective-permute-start.4 = (f32[1,128]{1,0:T(1,128)S(1)}, f32[1,128]{1,0:T(1,128)S(1)}, u32[]{:S(2)}, u32[]{:S(2)}) collective-permute-start(f32[1,128]{1,0:T(1,128)S(1)} %bitcast.11), channel_id=1, source_target_pairs={{0,8},{8,16},{16,24},{24,0},{1,9},{9,17},{17,25},{25,1},{2,10},{10... | collective-permute-start | bytes 1544 | tf_op jit(solution)/shard_map/ppermute | solution.py:341
  147.7 16.0 %collective-permute-start.5 = (f32[1,128]{1,0:T(1,128)S(1)}, f32[1,128]{1,0:T(1,128)S(1)}, u32[]{:S(2)}, u32[]{:S(2)}) collective-permute-start(f32[1,128]{1,0:T(1,128)S(1)} %bitcast.12), channel_id=1, source_target_pairs={{0,16},{8,24},{16,0},{24,8},{1,17},{9,25},{17,1},{25,9},{2,18},{10... | collective-permute-start | bytes 1544 | tf_op jit(solution)/shard_map/ppermute | solution.py:341
  150.2 14.2 %collective-permute-start.6 = (f32[1,128]{1,0:T(1,128)S(1)}, f32[1,128]{1,0:T(1,128)S(1)}, u32[]{:S(2)}, u32[]{:S(2)}) collective-permute-start(f32[1,128]{1,0:T(1,128)S(1)} %bitcast.13), channel_id=1, source_target_pairs={{0,24},{8,0},{16,8},{24,16},{1,25},{9,1},{17,9},{25,17},{2,26},{10... | collective-permute-start | bytes 1544 | tf_op jit(solution)/shard_map/ppermute | solution.py:341
